TPU v7x, 32 devices: a whole 2x2x4 slice. The times are simulated.
32 devices in a mesh: inst: 4 (over z), tp: 8 (over y, x, core).
Axes of the slice: x: 2, y: 2, z: 4, core: 2. Of those that a mesh axis runs over, the one named last changes fastest.
Arguments:
- x_steps: bfloat16 [2, 256, 8192], P(None, 'inst', 'tp'), may hold values from -6 to 6
- norm_gain: float32 [8192], replicated, may hold values from 0.1 to 1.9
- w_query: bfloat16 [8192, 8192], P(None, 'tp'), may hold values from -0.0625 to 0.0625
- w_keyval: bfloat16 [8192, 2048], P(None, 'tp'), may hold values from -0.0625 to 0.0625
- w_out: bfloat16 [8192, 8192], P('tp'), may hold values from -0.375 to 0.375
- key_cache: bfloat16 [256, 8, 128, 256], P('inst', 'tp')
- lengths: int32 [256], replicated, may hold values from 1 to 128, as said below
- moved_slots: int32 [4, 8], replicated, may hold values from 0 to 63, as said below
- partner_mask: int32 [8], replicated, may hold values from 1 to 3
Outputs:
- attention_out: bfloat16 [2, 256, 8192], P(None, 'inst', 'tp')
- arrived: bfloat16 [32, 8, 128, 256], P('inst', 'tp')
Inputs may be any that keep to these rules, and one draw needn't show every extreme that they name: `lengths`: some request has 128 cached tokens and some has 1. `moved_slots`: the 8 slots of one instance are distinct.
All inputs are finite; a program needn't handle non-finite values.
Results may differ from a plain program's by a relative error of at most 0.012.
The roundings to bfloat16 on the way count: a program that leaves them out, or rounds other values in their place, can miss the bound.
Values may be sent and summed in bfloat16 or wider, within the bound.
A program may use at most 128 MiB of HBM per device.

v0:
```python
from functools import reduce
import math

import jax
import jax.numpy as jnp
from jax import lax
from jax.sharding import PartitionSpec as P

KVH = 8


eps_norm = 1e-05
rope_base = 500000.0
floor_score = -1e30


def from_partner(block, axis, bit):
    count = lax.axis_size(axis)
    route = []
    for low in range(count):
        high = low | 1 << bit
        if high != low and high < count:
            route += [(low, high), (high, low)]
    return lax.ppermute(block, axis, route)


def as_sent(value):

    def short(part):
        return part.astype(jnp.bfloat16) if part.dtype == jnp.float32 else part

    return jax.tree.map(short, value)


def rotary(vectors, positions):
    half_dim = vectors.shape[-1] // 2
    frequency = rope_base ** (-(jnp.arange(half_dim, dtype=jnp.float32) * 2.0) / vectors.shape[-1])
    angles = positions.astype(jnp.float32)[..., None] * frequency
    cosine = jnp.cos(angles)[..., None, :]
    sine_part = jnp.sin(angles)[..., None, :]
    first_half = vectors[..., :half_dim]
    second_half = vectors[..., half_dim:]
    return jnp.concatenate(
        [
            first_half * cosine - second_half * sine_part,
            second_half * cosine + first_half * sine_part,
        ],
        -1,
    )


def block_terms(queries, block, start, length_rows):
    head_dim = queries.shape[-1]
    block_len = block.shape[1]
    scores = jnp.einsum(
        "rhd,rtd->rht", queries, block[..., :head_dim], preferred_element_type=jnp.float32
    ) / math.sqrt(head_dim)
    places = start + jnp.arange(block_len, dtype=jnp.int32)
    visible = (places[None, :] < length_rows[:, None])[:, None, :]
    scores = jnp.where(visible, scores, floor_score)
    block_max = jnp.max(scores, -1)
    weights = jnp.where(visible, jnp.exp(scores - block_max[..., None]), 0.0).astype(jnp.bfloat16)
    block_sum = jnp.sum(weights.astype(jnp.float32), -1)
    block_mix = jnp.einsum(
        "rht,rtd->rhd", weights, block[..., head_dim:], preferred_element_type=jnp.float32
    )
    return (block_max, block_sum, block_mix)


def fresh_terms(queries, fresh_kv):
    head_dim = queries.shape[-1]
    score = jnp.einsum(
        "rhd,rd->rh", queries, fresh_kv[:, :head_dim], preferred_element_type=jnp.float32
    ) / math.sqrt(head_dim)
    block_mix = jnp.broadcast_to(fresh_kv[:, None, head_dim:].astype(jnp.float32), queries.shape)
    return (score, jnp.ones_like(score), block_mix)


def combine(pieces):
    overall_max = reduce(jnp.maximum, [piece[0] for piece in pieces])
    numerator = reduce(
        jnp.add, [jnp.exp(piece[0] - overall_max)[..., None] * piece[2] for piece in pieces]
    )
    denominator = reduce(jnp.add, [jnp.exp(piece[0] - overall_max) * piece[1] for piece in pieces])
    return numerator / denominator[..., None]


def shards(
    x_steps, norm_gain, w_query, w_keyval, w_out, key_cache, lengths, moved_slots, partner_mask
):
    row_count = x_steps.shape[1]
    head_dim = key_cache.shape[-1] // 2
    block_len = key_cache.shape[2]
    group_size = lax.axis_size("tp") // KVH
    group_bits = group_size.bit_length() - 1
    member = lax.axis_index("tp") % group_size
    instance = lax.axis_index("inst")
    own_heads = w_query.shape[1] // head_dim
    own_lengths = lax.dynamic_slice_in_dim(lengths, instance * row_count, row_count)

    def collect(value, swapper):
        stacked = jax.tree.map(lambda leaf: leaf[None], value)
        for bit_index in range(group_bits):
            received = swapper(stacked, bit_index)
            low_side = member >> bit_index & 1 == 0
            stacked = jax.tree.map(
                lambda mine_part, their_part: jnp.where(
                    low_side,
                    jnp.concatenate([mine_part, their_part], 0),
                    jnp.concatenate([their_part, mine_part], 0),
                ),
                stacked,
                received,
            )
        return stacked

    def decode(step_index, positions, cache_rows, length_rows, earlier):
        gathered = lax.all_gather(x_steps[step_index], "tp", axis=1, tiled=True)
        widened = gathered.astype(jnp.float32)
        normed = (
            widened
            * lax.rsqrt(jnp.mean(widened * widened, -1, keepdims=True) + eps_norm)
            * norm_gain
        ).astype(jnp.bfloat16)
        query_raw = jnp.dot(normed, w_query, preferred_element_type=jnp.float32)
        keyval_raw = jnp.dot(normed, w_keyval, preferred_element_type=jnp.float32)
        joined = collect(
            jnp.concatenate([query_raw, keyval_raw], 1),
            lambda value, bit_index: from_partner(value, "tp", bit_index),
        )
        query_width = own_heads * head_dim
        query_all = jnp.moveaxis(joined[:, :, :query_width], 0, 1).reshape(
            row_count, group_size * own_heads, head_dim
        )
        keyval = jnp.moveaxis(joined[:, :, query_width:], 0, 1).reshape(row_count, 2 * head_dim)
        queries = rotary(query_all, positions).astype(jnp.bfloat16)
        partial_value = block_terms(queries, cache_rows[:, 0], member * block_len, length_rows)
        shared = collect(
            partial_value, lambda value, bit_index: from_partner(value, "tp", bit_index)
        )
        own_queries = lax.dynamic_slice_in_dim(queries, member * own_heads, own_heads, 1)
        pieces = [
            tuple(
                (
                    lax.dynamic_slice_in_dim(
                        member_part[block_index], member * own_heads, own_heads, 1
                    )
                    for member_part in shared
                )
            )
            for block_index in range(group_size)
        ]
        fresh_kv = jnp.concatenate(
            [rotary(keyval[:, None, :head_dim], positions)[:, 0], keyval[:, head_dim:]], -1
        ).astype(jnp.bfloat16)
        for fresh_item in earlier + [fresh_kv]:
            pieces.append(fresh_terms(own_queries, fresh_item))
        attended = combine(pieces).reshape(row_count, own_heads * head_dim).astype(jnp.bfloat16)
        head_terms = jnp.dot(attended, w_out, preferred_element_type=jnp.float32)
        return (
            lax.psum_scatter(head_terms, "tp", scatter_dimension=1, tiled=True).astype(
                jnp.bfloat16
            ),
            fresh_kv,
        )

    first_out, first_fresh = decode(0, own_lengths, key_cache, own_lengths, [])
    move_count = moved_slots.shape[1]
    move_ids = jnp.arange(move_count, dtype=jnp.int32)
    partner = jnp.bitwise_xor(instance, partner_mask)
    slots_self = moved_slots[instance]
    slots_partner = moved_slots[partner, move_ids]
    payload = (key_cache[slots_self], first_fresh[slots_self])
    moving = payload
    for bit_index in range(lax.axis_size("inst").bit_length() - 1):
        received = jax.tree.map(
            lambda part, own: part.astype(own.dtype),
            from_partner(as_sent(moving), "inst", bit_index),
            moving,
        )
        use_swap = partner_mask >> bit_index & 1 == 1
        moving = jax.tree.map(
            lambda their_part, mine_part: jnp.where(
                use_swap.reshape((move_count,) + (1,) * (mine_part.ndim - 1)), their_part, mine_part
            ),
            received,
            moving,
        )
    arrived_rows, arrived_fresh = moving
    cache_next = key_cache.at[slots_self].set(arrived_rows)
    fresh_next = first_fresh.at[slots_self].set(arrived_fresh)
    length_next = own_lengths.at[slots_self].set(lengths[partner * row_count + slots_partner])
    second_out, unused = decode(1, length_next + 1, cache_next, length_next, [fresh_next])
    return (jnp.stack([first_out, second_out]), arrived_rows)


def solution(mesh):
    placed = (
        P(None, "inst", "tp"),
        P(),
        P(None, "tp"),
        P(None, "tp"),
        P("tp", None),
        P("inst", "tp", None, None),
        P(),
        P(),
        P(),
    )
    return jax.shard_map(
        shards,
        mesh=mesh,
        in_specs=placed,
        out_specs=(P(None, "inst", "tp"), P("inst", "tp", None, None)),
        check_vma=False,
    )
```

profile of v0, /device:TPU:0, one launch (start us, length us, event | category | flops | bytes accessed | tf_op | source)
XLA Modules:
  0.0 197.3 jit_solution(2555894529497404274)
XLA Ops:
  7.2 4.7 %copy.41 = bf16[64,1,128,256]{3,2,1,0:T(8,128)(2,1)} copy(bf16[64,1,128,256]{3,2,1,0:T(8,128)(2,1)} %param.14) | data formatting | bytes 8388608
  11.9 0.7 fusion.111
  12.7 2.8 %gather_fusion.2 = bf16[8,128,256]{2,1,0:T(8,128)(2,1)S(1)} fusion(bf16[64,128,256]{2,1,0:T(8,128)(2,1)} %bitcast.87, s32[1024]{0:T(1024)S(1)} %pad_clamp_fusion), kind=kCustom, calls=%fused_computation.2 | custom fusion | bytes 1048608 | tf_op jit(solution)/shard_map/gather | solution.py:173
  15.5 3.1 %collective-permute-start = (bf16[8,1,128,256]{3,2,0,1:T(8,128)(2,1)S(1)}, bf16[8,1,128,256]{3,2,0,1:T(8,128)(2,1)S(1)}, u32[]{:S(2)}, u32[]{:S(2)}) collective-permute-start(bf16[8,1,128,256]{3,2,0,1:T(8,128)(2,1)S(1)} %bitcast.93), channel_id=1, source_target_pairs={{0,8},{8,0},{16,24},{24,16},{1,9},{9,1},{17,25},{25,17},{2,10},{10... | collective-permute-start | bytes 1572872 | tf_op jit(solution)/shard_map/ppermute | solution.py:24
  18.7 0.7 gather_fusion
  19.4 0.1 fusion.110
  19.5 0.1 iota_compare_fusion.1
  19.6 0.6 gather_fusion.1
  20.2 0.6 scatter_fusion
  20.8 9.7 %collective-permute-done = bf16[8,1,128,256]{3,2,0,1:T(8,128)(2,1)S(1)} collective-permute-done((bf16[8,1,128,256]{3,2,0,1:T(8,128)(2,1)S(1)}, bf16[8,1,128,256]{3,2,0,1:T(8,128)(2,1)S(1)}, u32[]{:S(2)}, u32[]{:S(2)}) %collective-permute-start) | collective-permute-done | bytes 524320 | tf_op jit(solution)/shard_map/ppermute | solution.py:24
  30.5 0.1 broadcast_select_fusion
  30.7 2.8 %collective-permute-start.1 = (bf16[8,1,128,256]{3,2,0,1:T(8,128)(2,1)S(1)}, bf16[8,1,128,256]{3,2,0,1:T(8,128)(2,1)S(1)}, u32[]{:S(2)}, u32[]{:S(2)}) collective-permute-start(bf16[8,1,128,256]{3,2,0,1:T(8,128)(2,1)S(1)} %broadcast_select_fusion), channel_id=1, source_target_pairs={{0,16},{16,0},{8,24},{24,8},{1,17},{17,1},{9,25},{25,9},{2,18},{18... | collective-permute-start | bytes 1572872 | tf_op jit(solution)/shard_map/ppermute | solution.py:24
  33.6 0.3 multiply_cosine_fusion.3
  33.9 22.1 %collective-permute-done.1 = bf16[8,1,128,256]{3,2,0,1:T(8,128)(2,1)S(1)} collective-permute-done((bf16[8,1,128,256]{3,2,0,1:T(8,128)(2,1)S(1)}, bf16[8,1,128,256]{3,2,0,1:T(8,128)(2,1)S(1)}, u32[]{:S(2)}, u32[]{:S(2)}) %collective-permute-start.1) | collective-permute-done | bytes 524320 | tf_op jit(solution)/shard_map/ppermute | solution.py:24
  56.0 0.9 fusion.105
  56.9 1.6 fusion
  58.5 9.4 %fusion.59 = f32[64,1024]{1,0:T(8,128)S(1)} fusion(bf16[8192,1024]{1,0:T(8,128)(2,1)} %param.11, bf16[1,64,8192]{2,1,0:T(8,128)(2,1)} %all-gather.5.cloned.1.call-done, f32[8192]{0:T(1024)S(1)} %copy-done.6, f32[64]{0:T(128)S(1)} %add_rsqrt_fusion.1), kind=kOutput, calls=%fused_computation.45 | convolution fusion | flops 1075838976 | bytes 18120960 | tf_op jit(solution)/shard_map/dot_general | solution.py:125
  68.0 0.9 fusion.57
  69.0 1.5 fusion.3
  70.6 3.5 %fusion.53 = f32[64,256]{1,0:T(8,128)S(1)} fusion(bf16[8192,256]{1,0:T(8,128)(2,1)} %param.12, bf16[1,64,8192]{2,1,0:T(8,128)(2,1)} %all-gather.7.cloned.1.call-done, f32[64]{0:T(128)S(1)} %add_rsqrt_fusion, f32[8192]{0:T(1024)S(1)} %copy-done.6), kind=kOutput, calls=%fused_computation.42 | convolution fusion | flops 270532608 | bytes 5341440 | tf_op jit(solution)/shard_map/dot_general | solution.py:126
  74.1 8.9 %fusion.55 = f32[64,1024]{1,0:T(8,128)S(1)} fusion(bf16[8192,1024]{1,0:T(8,128)(2,1)} %param.11, bf16[1,64,8192]{2,1,0:T(8,128)(2,1)S(1)} %copy-done.5, f32[64]{0:T(128)S(1)} %add_rsqrt_fusion, f32[8192]{0:T(1024)S(1)} %copy-done.6), kind=kOutput, calls=%fused_computation.43 | convolution fusion | flops 1075838976 | bytes 18120960 | tf_op jit(solution)/shard_map/dot_general | solution.py:125
  83.2 0.3 fusion.80
  83.5 0.1 fusion.95
  83.6 0.6 gather_fusion.3
  84.2 0.6 collective-permute-start.2
  84.8 0.2 subtract_convert_fusion.1
  85.0 3.0 %fusion.113 = (f32[64,8]{1,0:T(8,128)S(1)}, f32[64,8,128]{2,1,0:T(8,128)S(1)}) fusion(bf16[64,128,256]{2,1,0:T(8,128)(2,1)} %bitcast.88, bf16[64,8,64]{2,1,0:T(8,128)(2,1)S(1)} %get-tuple-element.20, bf16[64,8,64]{2,1,0:T(8,128)(2,1)S(1)} %get-tuple-element.19, pred[64,128]{1,0:T(8,128)(4,1)S(1)} %iota_compare_fusion.1), kind=kOutput, calls=%fused_computation.152 | convolution fusion | flops 17235456 | bytes 2500608 | tf_op jit(solution)/shard_map/rhd,rtd->rht/dot_general | solution.py:55
  88.0 0.3 fusion.89
  88.3 0.2 convert_reduce_fusion.1
  88.6 0.7 fusion.47
  89.3 2.5 %scatter_fusion.1 = bf16[64,128,256]{2,1,0:T(8,128)(2,1)} fusion(bf16[64,128,256]{2,1,0:T(8,128)(2,1)} %bitcast.89, s32[8]{0:T(128)S(1)} %fusion.97, bf16[8,128,256]{2,1,0:T(8,128)(2,1)S(1)} %get-tuple-element.18), kind=kCustom, calls=%fused_computation.5 | custom fusion | bytes 1572896 | tf_op jit(solution)/shard_map/scatter | solution.py:190
  91.8 10.1 %fusion.64 = f32[64,8192]{1,0:T(8,128)} fusion(bf16[1024,8192]{1,0:T(8,128)(2,1)} %param.13, bf16[8,8,8,128]{3,2,1,0:T(8,128)(2,1)S(1)} %bitcast.94), kind=kOutput, calls=%fused_computation.60 | convolution fusion | flops 1073741824 | bytes 19005440 | tf_op jit(solution)/shard_map/dot_general | solution.py:159
  102.0 0.2 reduce-scatter.5.cloned.1.call-start
  102.2 0.2 subtract_convert_fusion
  102.4 2.9 %fusion.112 = (f32[64,8]{1,0:T(8,128)S(1)}, f32[64,8,128]{2,1,0:T(8,128)S(1)}) fusion(bf16[64,128,256]{2,1,0:T(8,128)(2,1)} %scatter_fusion.1, bf16[64,8,64]{2,1,0:T(8,128)(2,1)S(1)} %get-tuple-element.22, bf16[64,8,64]{2,1,0:T(8,128)(2,1)S(1)} %get-tuple-element.21, pred[64,128]{1,0:T(8,128)(4,1)S(1)} %iota_compare_fusion), kind=kOutput, calls=%fused_computation.151 | convolution fusion | flops 17235456 | bytes 2500608 | tf_op jit(solution)/shard_map/rhd,rtd->rht/dot_general | solution.py:55
  105.3 0.3 fusion.85
  105.6 3.3 %collective-permute-start.3 = (bf16[8,256]{1,0:T(8,128)(2,1)S(1)}, bf16[8,256]{1,0:T(8,128)(2,1)S(1)}, u32[]{:S(2)}, u32[]{:S(2)}) collective-permute-start(bf16[8,256]{1,0:T(8,128)(2,1)S(1)} %broadcast_select_fusion.2), channel_id=1, source_target_pairs={{0,16},{16,0},{8,24},{24,8},{1,17},{17,1},{9,25},{25,9},{2,18},{18... | collective-permute-start | bytes 12296 | tf_op jit(solution)/shard_map/ppermute | solution.py:24
  108.9 0.2 convert_reduce_fusion
  109.1 1.4 collective-permute-done.3
  110.5 0.7 scatter_custom_fusion.2
  111.2 0.3 fusion.87
  111.5 2.4 %fusion.50 = bf16[64,8,128]{2,1,0:T(8,128)(2,1)S(1)} fusion(bf16[64,128,256]{2,1,0:T(8,128)(2,1)} %scatter_fusion.1, f32[64,8]{1,0:T(8,128)S(1)} %get-tuple-element.11, f32[64,128]{1,0:T(8,128)S(1)} %fusion.91, f32[64,8]{1,0:T(8,128)S(1)} %get-tuple-element.14, f32[64,128]{1,0:T(8,128)S(1)} %get-tuple-element.31, f32[64,8]{1,0:T(8,128)S(1)} %get-tuple-element.13, ...), kind=kOutput, calls=%fused_computation.37 | convolution fusion | flops 17432576 | bytes 2574336 | tf_op jit(solution)/shard_map/rht,rtd->rhd/dot_general | solution.py:64
  114.0 10.3 %fusion.61 = f32[64,8192]{1,0:T(8,128)} fusion(bf16[1024,8192]{1,0:T(8,128)(2,1)} %param.13, bf16[8,8,8,128]{3,2,1,0:T(8,128)(2,1)S(1)} %bitcast.95), kind=kOutput, calls=%fused_computation.57 | convolution fusion | flops 1073741824 | bytes 19005440 | tf_op jit(solution)/shard_map/dot_general | solution.py:159
  124.3 20.0 %reduce-scatter.3.cloned.1.call-done = f32[64,1024]{1,0:T(8,128)} async-done(((f32[64,8192]{1,0:T(8,128)}), f32[64,1024]{1,0:T(8,128)}) %reduce-scatter.3.cloned.1.call-update) | async-done | bytes 262160 | tf_op jit(solution)/shard_map/reduce_scatter | solution.py:161
  144.3 1.0 convert_bitcast_fusion.1
  145.2 43.8 %reduce-scatter.5.cloned.1.call-done = f32[64,1024]{1,0:T(8,128)} async-done(((f32[64,8192]{1,0:T(8,128)}), f32[64,1024]{1,0:T(8,128)}) %reduce-scatter.5.cloned.1.call-update) | async-done | bytes 262160 | tf_op jit(solution)/shard_map/reduce_scatter | solution.py:161
  189.0 1.0 convert_bitcast_fusion
  190.0 0.7 pad_maximum_fusion
  (56 shorter events, 0.8 us)
Async XLA Ops:
  7.2 4.7 %copy-start.7 = (bf16[2,64,1024]{2,1,0:T(8,128)(2,1)S(1)}, bf16[2,64,1024]{2,1,0:T(8,128)(2,1)}, u32[]{:S(2)}) copy-start(bf16[2,64,1024]{2,1,0:T(8,128)(2,1)} %param.9) | copy-start | bytes 786436
  7.2 5.5 %copy-start.1 = (s32[4,8]{1,0:T(4,128)S(1)}, s32[4,8]{1,0:T(4,128)}, u32[]{:S(2)}) copy-start(s32[4,8]{1,0:T(4,128)} %param.16) | copy-start | bytes 388
  7.2 11.5 %copy-start.8 = (s32[8]{0:T(128)S(1)}, s32[8]{0:T(128)}, u32[]{:S(2)}) copy-start(s32[8]{0:T(128)} %param.17) | copy-start | bytes 100
  7.2 49.7 %all-gather.5.cloned.1.call-start = ((), (), s32[]{:S(2)}) async-start(), calls=%async_computation.4 | async-start | bytes 1179648 | tf_op jit(solution)/shard_map/all_gather | solution.py:118
  11.9 7.5 %copy-start = (s32[256]{0:T(256)S(1)}, s32[256]{0:T(256)}, u32[]{:S(2)}) copy-start(s32[256]{0:T(256)} %param.15) | copy-start | bytes 3076
  12.7 56.4 %all-gather.7.cloned.1.call-start = ((), (), s32[]{:S(2)}) async-start(), calls=%async_computation.5 | async-start | bytes 1179648 | tf_op jit(solution)/shard_map/all_gather | solution.py:118
  15.5 15.0 %collective-permute-start = (bf16[8,1,128,256]{3,2,0,1:T(8,128)(2,1)S(1)}, bf16[8,1,128,256]{3,2,0,1:T(8,128)(2,1)S(1)}, u32[]{:S(2)}, u32[]{:S(2)}) collective-permute-start(bf16[8,1,128,256]{3,2,0,1:T(8,128)(2,1)S(1)} %bitcast.93), channel_id=1, source_target_pairs={{0,8},{8,0},{16,24},{24,16},{1,9},{9,1},{17,25},{25,17},{2,10},{10... | collective-permute-start | bytes 1572872 | tf_op jit(solution)/shard_map/ppermute | solution.py:24
  18.6 125.6 %reduce-scatter.3.cloned.1.call-start = ((), (), s32[]{:S(2)}) async-start(), calls=%async_computation.2 | async-start | bytes 2359296 | tf_op jit(solution)/shard_map/reduce_scatter | solution.py:161
  30.5 28.0 %copy-start.6 = (f32[8192]{0:T(1024)S(1)}, f32[8192]{0:T(1024)}, u32[]{:S(2)}) copy-start(f32[8192]{0:T(1024)} %param.10) | copy-start | bytes 98308
  30.7 25.3 %collective-permute-start.1 = (bf16[8,1,128,256]{3,2,0,1:T(8,128)(2,1)S(1)}, bf16[8,1,128,256]{3,2,0,1:T(8,128)(2,1)S(1)}, u32[]{:S(2)}, u32[]{:S(2)}) collective-permute-start(bf16[8,1,128,256]{3,2,0,1:T(8,128)(2,1)S(1)} %broadcast_select_fusion), channel_id=1, source_target_pairs={{0,16},{16,0},{8,24},{24,8},{1,17},{17,1},{9,25},{25,9},{2,18},{18... | collective-permute-start | bytes 1572872 | tf_op jit(solution)/shard_map/ppermute | solution.py:24
  58.5 9.4 %copy-start.3 = (bf16[8192,256]{1,0:T(8,128)(2,1)S(1)}, bf16[8192,256]{1,0:T(8,128)(2,1)}, u32[]{:S(2)}) copy-start(bf16[8192,256]{1,0:T(8,128)(2,1)} %param.12) | copy-start | bytes 12582916
  58.5 9.4 %copy-start.4 = (bf16[1,64,8192]{2,1,0:T(8,128)(2,1)S(1)}, bf16[1,64,8192]{2,1,0:T(8,128)(2,1)}, u32[]{:S(2)}) copy-start(bf16[1,64,8192]{2,1,0:T(8,128)(2,1)} %all-gather.5.cloned.1.call-done) | copy-start | bytes 3145732
  70.6 3.5 %copy-start.5 = (bf16[1,64,8192]{2,1,0:T(8,128)(2,1)S(1)}, bf16[1,64,8192]{2,1,0:T(8,128)(2,1)}, u32[]{:S(2)}) copy-start(bf16[1,64,8192]{2,1,0:T(8,128)(2,1)} %all-gather.7.cloned.1.call-done) | copy-start | bytes 3145732
  84.2 21.4 %collective-permute-start.2 = (bf16[8,256]{1,0:T(8,128)(2,1)S(1)}, bf16[8,256]{1,0:T(8,128)(2,1)S(1)}, u32[]{:S(2)}, u32[]{:S(2)}) collective-permute-start(bf16[8,256]{1,0:T(8,128)(2,1)S(1)} %gather_fusion.3), channel_id=1, source_target_pairs={{0,8},{8,0},{16,24},{24,16},{1,9},{9,1},{17,25},{25,17},{2,10},{10... | collective-permute-start | bytes 12296 | tf_op jit(solution)/shard_map/ppermute | solution.py:24
  84.8 3.8 %copy-start.2 = (bf16[64,1,128,256]{3,2,1,0:T(8,128)(2,1)S(1)}, bf16[64,1,128,256]{3,2,1,0:T(8,128)(2,1)}, u32[]{:S(2)}) copy-start(bf16[64,1,128,256]{3,2,1,0:T(8,128)(2,1)} %copy.41) | copy-start | bytes 12582916
  102.0 87.1 %reduce-scatter.5.cloned.1.call-start = ((), (), s32[]{:S(2)}) async-start(), calls=%async_computation.3 | async-start | bytes 2359296 | tf_op jit(solution)/shard_map/reduce_scatter | solution.py:161
  105.6 4.9 %collective-permute-start.3 = (bf16[8,256]{1,0:T(8,128)(2,1)S(1)}, bf16[8,256]{1,0:T(8,128)(2,1)S(1)}, u32[]{:S(2)}, u32[]{:S(2)}) collective-permute-start(bf16[8,256]{1,0:T(8,128)(2,1)S(1)} %broadcast_select_fusion.2), channel_id=1, source_target_pairs={{0,16},{16,0},{8,24},{24,8},{1,17},{17,1},{9,25},{25,9},{2,18},{18... | collective-permute-start | bytes 12296 | tf_op jit(solution)/shard_map/ppermute | solution.py:24
Sparse Core Ops, SparseCore 0:
  12.8 26.1 all-gather.4
  40.9 23.4 all-gather.6
  102.1 42.1 reduce-scatter.2
  147.8 41.2 reduce-scatter.4
where the time goes:
time: 198 us; the launch traced here: 197 us
  waiting for transfers between devices  97 us (49%)
  matrix products  53 us (27%)
  between operations  14.2 us (7%)
  local copies, waits for them, and re-layouts  13.3 us (7%)
  starting transfers between devices  10.2 us (5%)
  other arithmetic  9.54 us (5%)
    reduce_scatter x2, waiting for transfers between devices, decode(): lax.psum_scatter(head_terms, 'tp', scatter_dimension=1, tiled=True)  63.7 us
    ppermute x4, waiting for transfers between devices, from_partner(): return lax.ppermute(block, axis, route)  33.1 us
    dot_general x2, matrix products, decode(): head_terms = jnp.dot(attended, w_out, preferred_element_type=jnp.float32)  20.4 us
    dot_general x2, matrix products, decode(): query_raw = jnp.dot(normed, w_query, preferred_element_type=jnp.float32)  18.3 us
    ppermute x4, starting transfers between devices, from_partner(): return lax.ppermute(block, axis, route)  9.83 us
    dot_general x2, matrix products, block_terms(): jnp.einsum('rhd,rtd->rht', queries, block[..., :head_dim], preferred_elem...  5.94 us
    unnamed x23, local copies, waits for them, and re-layouts  4.84 us
    dot_general x2, matrix products, decode(): keyval_raw = jnp.dot(normed, w_keyval, preferred_element_type=jnp.float32)  4.37 us
  transfers between devices with their start and end apart: 8, of which 5 were waited for; matrix products, arithmetic and copies ran while one was open for 27% of the time, Pallas kernels for 0%

commit v1 on v0

--- a/solution.py
+++ b/solution.py
@@ -4,6 +4,8 @@
 import jax
 import jax.numpy as jnp
 from jax import lax
+from jax.experimental import pallas as pl
+from jax.experimental.pallas import tpu as pltpu
 from jax.sharding import PartitionSpec as P
 
 KVH = 8
@@ -194,6 +196,542 @@
     return (jnp.stack([first_out, second_out]), arrived_rows)
 
 
+def fused_kernel(
+    len_ref,
+    slot_ref,
+    mask_ref,
+    x_ref,
+    gain_ref,
+    wq_hbm,
+    wkv_hbm,
+    wo_hbm,
+    cache_hbm,
+    out_ref,
+    arrived_ref,
+    wq,
+    wkv,
+    wo,
+    cache,
+    xg,
+    acc,
+    square,
+    place,
+    qs,
+    fresh,
+    mixed,
+    attended,
+    leave,
+    mid_in,
+    mid,
+    last_in,
+    fsend,
+    frecv,
+    sib_send,
+    sib_recv,
+    own,
+    first_send,
+    first_recv,
+    second_send,
+    second_recv,
+    late_mixed,
+    late_send,
+    late_recv,
+    load_sem,
+    gather_send,
+    gather_recv,
+    move_send,
+    move_recv,
+    fresh_send,
+    fresh_recv,
+    sum_send,
+    sum_recv,
+    late_send_sem,
+    late_recv_sem,
+):
+    tp = lax.axis_index("tp")
+    inst = lax.axis_index("inst")
+    rows = x_ref.shape[1]
+    width = x_ref.shape[2]
+    moves = slot_ref.shape[1]
+    hd = cache.shape[-1] // 2
+    heads = qs.shape[1] // 2
+    scale = 1.0 / math.sqrt(hd)
+
+    def remote(src, dst, send, recv, **where):
+        return pltpu.make_async_remote_copy(
+            src_ref=src,
+            dst_ref=dst,
+            send_sem=send,
+            recv_sem=recv,
+            device_id=where,
+            device_id_type=pl.DeviceIdType.MESH,
+        )
+
+    cache_load = pltpu.make_async_copy(cache_hbm, cache, load_sem.at[24])
+    cache_load.start()
+    weight_loads = []
+    for i in range(8):
+        start = pl.multiple_of((tp ^ i) * width, width)
+        pair = (
+            pltpu.make_async_copy(wq_hbm.at[pl.ds(start, width), :], wq.at[i], load_sem.at[i]),
+            pltpu.make_async_copy(
+                wkv_hbm.at[pl.ds(start, width), :], wkv.at[i], load_sem.at[8 + i]
+            ),
+        )
+        for load in pair:
+            load.start()
+        weight_loads.append(pair)
+    out_order = (1, 3, 5, 7, 2, 6, 4, 0)
+    out_loads = {}
+    for i in out_order:
+        start = pl.multiple_of((tp ^ i) * width, width)
+        out_loads[i] = pltpu.make_async_copy(
+            wo_hbm.at[:, pl.ds(start, width)], wo.at[i], load_sem.at[16 + i]
+        )
+        out_loads[i].start()
+
+    barrier = pltpu.get_barrier_semaphore()
+    for i in range(1, 8):
+        pl.semaphore_signal(
+            barrier, inc=1, device_id={"tp": tp ^ i}, device_id_type=pl.DeviceIdType.MESH
+        )
+    for i in range(1, 4):
+        pl.semaphore_signal(
+            barrier, inc=1, device_id={"inst": inst ^ i}, device_id_type=pl.DeviceIdType.MESH
+        )
+    xg[0] = x_ref[...]
+    pl.semaphore_wait(barrier, 10)
+
+    def feature_copy(k, src, dst, to, part=None):
+        src_ref = xg.at[src] if part is None else xg.at[src, part]
+        dst_ref = xg.at[dst] if part is None else xg.at[dst, part]
+        return remote(src_ref, dst_ref, gather_send.at[k], gather_recv.at[k], tp=tp ^ to)
+
+    along_x = [feature_copy(0, 0, 2, 2, 0), feature_copy(1, 0, 2, 2, 1)]
+    along_y = [feature_copy(2, 0, 4, 4, 1), feature_copy(3, 0, 4, 4, 0)]
+    to_sibling = [feature_copy(6, 0, 1, 1)]
+    along_x[0].start()
+    along_y[0].start()
+    along_x[1].start()
+    along_y[1].start()
+    to_sibling[0].start()
+
+    cache_load.wait()
+    move_bits = [(1, 2) if j < moves // 2 else (2, 1) for j in range(moves)]
+    first_moves = []
+    for j in range(moves):
+        leave[j] = cache[slot_ref[inst, j]]
+        move = remote(
+            leave.at[j], mid_in.at[j], move_send.at[j], move_recv.at[j], inst=inst ^ move_bits[j][0]
+        )
+        move.start()
+        first_moves.append(move)
+
+    @pl.loop(0, rows)
+    def _(r):
+        level = jnp.full((1, 2 * hd), len_ref[inst * rows + r], jnp.int32)
+        place[pl.ds(r, 1), :] = level[:, :hd]
+
+    row_ids = lax.broadcasted_iota(jnp.int32, (rows, hd), 0)
+    own_place = place[...]
+    next_place = own_place
+    moved_len = []
+    for j in range(moves):
+        partner = inst ^ mask_ref[j]
+        length = len_ref[partner * rows + slot_ref[partner, j]]
+        moved_len.append(length)
+        next_place = jnp.where(row_ids == slot_ref[inst, j], length, next_place)
+    positions = jnp.concatenate([own_place, next_place + 1], 0).astype(jnp.float32)
+    lane = lax.broadcasted_iota(jnp.int32, (1, hd), 1)
+    pair_id = jnp.where(lane < hd // 2, lane, lane - hd // 2).astype(jnp.float32)
+    frequency = jnp.exp(pair_id * (-2.0 * math.log(rope_base) / hd))
+    angles = positions * frequency
+    cosine = jnp.cos(angles)
+    sine = jnp.sin(angles)
+    sine = jnp.where(lane < hd // 2, -sine, sine)
+
+    acc[...] = jnp.zeros_like(acc)
+    square[...] = jnp.zeros_like(square)
+    q_width = wq.shape[2]
+
+    def project(i):
+        for load in weight_loads[i]:
+            load.wait()
+        wide = xg[i].reshape(2 * rows, width).astype(jnp.float32)
+        square[...] += jnp.sum(wide * wide, -1, keepdims=True)
+        scaled = (wide * gain_ref[pl.ds(tp ^ i, 1), :]).astype(jnp.bfloat16)
+
+        @pl.loop(0, q_width // 256)
+        def _(c):
+            cols = pl.ds(pl.multiple_of(c * 256, 256), 256)
+            acc[:, cols] += jnp.dot(scaled, wq[i, :, cols], preferred_element_type=jnp.float32)
+
+        acc[:, q_width:] += jnp.dot(scaled, wkv[i], preferred_element_type=jnp.float32)
+
+    project(0)
+    along_x[0].wait_recv()
+    along_y[0].wait_recv()
+    across = [feature_copy(4, 2, 6, 4, 0), feature_copy(5, 4, 6, 2, 1)]
+    across[0].start()
+    across[1].start()
+    to_sibling[0].wait_recv()
+    project(1)
+    along_x[1].wait_recv()
+    to_sibling.append(feature_copy(7, 2, 3, 1))
+    to_sibling[1].start()
+    along_y[1].wait_recv()
+    to_sibling.append(feature_copy(8, 4, 5, 1))
+    to_sibling[2].start()
+    project(2)
+    project(4)
+    to_sibling[1].wait_recv()
+    project(3)
+    to_sibling[2].wait_recv()
+    project(5)
+    across[0].wait_recv()
+    across[1].wait_recv()
+    to_sibling.append(feature_copy(9, 6, 7, 1))
+    to_sibling[3].start()
+    project(6)
+    to_sibling[3].wait_recv()
+    project(7)
+
+    factor = lax.rsqrt(square[...] * (1.0 / (8 * width)) + eps_norm)
+
+    def turned(part):
+        part = part * factor
+        return (part * cosine + pltpu.roll(part, hd // 2, 1) * sine).astype(jnp.bfloat16)
+
+    for h in range(heads):
+        rotated = turned(acc[:, h * hd : (h + 1) * hd]).astype(jnp.float32)
+        qs[:, h, :] = rotated[:rows]
+        qs[:, heads + h, :] = rotated[rows:]
+    fresh[:, :hd] = turned(acc[:, q_width : q_width + hd]).astype(jnp.float32)
+    fresh[:, hd:] = (acc[:, q_width + hd :] * factor).astype(jnp.bfloat16).astype(jnp.float32)
+
+    for j in range(moves):
+        fsend[pl.ds(j, 1), :] = fresh[pl.ds(slot_ref[inst, j], 1), :]
+    fresh_moves = []
+    for i in range(1, 4):
+        move = remote(
+            fsend, frecv.at[i - 1], fresh_send.at[i - 1], fresh_recv.at[i - 1], inst=inst ^ i
+        )
+        move.start()
+        fresh_moves.append(move)
+
+    second_moves = []
+    for j in range(moves):
+        first_moves[j].wait_recv()
+        taken = (mask_ref[j] & move_bits[j][0]) != 0
+        mid[j] = jnp.where(taken, mid_in[j], leave[j])
+        move = remote(
+            mid.at[j],
+            last_in.at[j],
+            move_send.at[moves + j],
+            move_recv.at[moves + j],
+            inst=inst ^ move_bits[j][1],
+        )
+        move.start()
+        second_moves.append(move)
+
+    def attend(queries, keys, values, length, news):
+        score = scale * lax.dot_general(
+            queries.astype(jnp.bfloat16),
+            keys,
+            (((1,), (1,)), ((), ())),
+            preferred_element_type=jnp.float32,
+        )
+        visible = lax.broadcasted_iota(jnp.int32, score.shape, 1) < length
+        score = jnp.where(visible, score, floor_score)
+        top = jnp.max(score, -1, keepdims=True)
+        weights = jnp.where(visible, jnp.exp(score - top), 0.0).astype(jnp.bfloat16)
+        total = jnp.sum(weights.astype(jnp.float32), -1, keepdims=True)
+        mix = jnp.dot(weights, values, preferred_element_type=jnp.float32)
+        marks = []
+        overall = top
+        for row, allowed in news:
+            mark = scale * jnp.sum(queries * row[:, :hd], -1, keepdims=True)
+            if allowed is not None:
+                mark = jnp.where(allowed, mark, floor_score)
+            marks.append(mark)
+            overall = jnp.maximum(overall, mark)
+        share = jnp.exp(top - overall)
+        numerator = share * mix
+        denominator = share * total
+        for (row, allowed), mark in zip(news, marks):
+            share = jnp.exp(mark - overall)
+            if allowed is not None:
+                share = jnp.where(allowed, share, 0.0)
+            numerator = numerator + share * row[:, hd:]
+            denominator = denominator + share
+        return numerator / denominator
+
+    later = lax.broadcasted_iota(jnp.int32, (2 * heads, 1), 0) >= heads
+
+    @pl.loop(0, rows // 8)
+    def _(group):
+        for u in range(8):
+            r = group * 8 + u
+            mixed[r] = attend(
+                qs[r],
+                cache[r, :, :hd],
+                cache[r, :, hd:],
+                len_ref[inst * rows + r],
+                [(fresh[pl.ds(r, 1), :], None), (fresh[pl.ds(rows + r, 1), :], later)],
+            )
+
+    for h in range(heads):
+        cols = slice(h * hd, (h + 1) * hd)
+        attended[:rows, cols] = mixed[:, h, :].astype(jnp.bfloat16)
+        attended[rows:, cols] = mixed[:, heads + h, :].astype(jnp.bfloat16)
+
+    tile = 256
+
+    def column_loop(body):
+        @pl.loop(0, width // tile)
+        def _(c):
+            body(pl.ds(pl.multiple_of(c * tile, tile), tile))
+
+    def term(i, cols):
+        return jnp.dot(attended[...], wo[i, :, cols], preferred_element_type=jnp.float32)
+
+    sibling_sums = []
+    for i in (1, 3, 5, 7):
+        k = i // 2
+        out_loads[i].wait()
+
+        def body(cols):
+            sib_send[k, :, cols] = term(i, cols).astype(jnp.bfloat16)
+
+        column_loop(body)
+        copy = remote(
+            sib_send.at[k], sib_recv.at[k], sum_send.at[k], sum_recv.at[k], tp=tp ^ 1
+        )
+        copy.start()
+        sibling_sums.append(copy)
+
+    first_sums = [[None, None], [None, None]]
+
+    def send_first(s, n):
+        k = 4 + 2 * s + n
+        copy = remote(
+            first_send.at[s, n],
+            first_recv.at[s, n],
+            sum_send.at[k],
+            sum_recv.at[k],
+            tp=tp ^ (2, 4)[s],
+        )
+        copy.start()
+        first_sums[s][n] = copy
+
+    for i in (6, 2, 4, 0):
+        k = i // 2
+        out_loads[i].wait()
+        sibling_sums[k].wait_recv()
+
+        def body(cols):
+            chip = term(i, cols) + sib_recv[k, :, cols].astype(jnp.float32)
+            if i == 6:
+                first_send[0, 1, :, cols] = chip[:rows].astype(jnp.bfloat16)
+                first_send[1, 1, :, cols] = chip[rows:].astype(jnp.bfloat16)
+            elif i == 2:
+                first_send[0, 0, :, cols] = chip[:rows].astype(jnp.bfloat16)
+                own[1, :rows, cols] = chip[rows:]
+            elif i == 4:
+                own[1, rows:, cols] = chip[:rows]
+                first_send[1, 0, :, cols] = chip[rows:].astype(jnp.bfloat16)
+            else:
+                own[0, :, cols] = chip
+
+        column_loop(body)
+        if i == 6:
+            send_first(0, 1)
+            send_first(1, 1)
+        elif i == 2:
+            send_first(0, 0)
+        elif i == 4:
+            send_first(1, 0)
+
+    second_sums = []
+    for s in range(2):
+        first_sums[s][1].wait_recv()
+        base = own[1, rows:, :] if s == 0 else own[1, :rows, :]
+        second_send[s] = (base + first_recv[s, 1].astype(jnp.float32)).astype(jnp.bfloat16)
+        copy = remote(
+            second_send.at[s],
+            second_recv.at[s],
+            sum_send.at[8 + s],
+            sum_recv.at[8 + s],
+            tp=tp ^ (4, 2)[s],
+        )
+        copy.start()
+        second_sums.append(copy)
+
+    for move in fresh_moves:
+        move.wait_recv()
+    for j in range(moves):
+        second_moves[j].wait_recv()
+        taken = (mask_ref[j] & move_bits[j][1]) != 0
+        arrived_ref[j, 0] = jnp.where(taken, last_in[j], mid[j])
+    for j in range(moves):
+        mask = mask_ref[j]
+        carried = jnp.where(
+            mask == 1,
+            frecv[0, pl.ds(j, 1), :],
+            jnp.where(mask == 2, frecv[1, pl.ds(j, 1), :], frecv[2, pl.ds(j, 1), :]),
+        )
+        slot = slot_ref[inst, j]
+        late_mixed[j] = attend(
+            qs[slot],
+            arrived_ref[j, 0, :, :hd],
+            arrived_ref[j, 0, :, hd:],
+            moved_len[j],
+            [(carried, None), (fresh[pl.ds(rows + slot, 1), :], None)],
+        )
+    late = jnp.concatenate([late_mixed[:, heads + h, :] for h in range(heads)], -1)
+    late = late.astype(jnp.bfloat16)
+    late_copies = []
+    for i in (6, 7, 2, 3, 4, 5, 1, 0):
+
+        def body(cols):
+            late_send[i, :, cols] = jnp.dot(
+                late, wo[i, :, cols], preferred_element_type=jnp.float32
+            )
+
+        column_loop(body)
+        if i:
+            copy = remote(
+                late_send.at[i],
+                late_recv.at[i],
+                late_send_sem.at[i],
+                late_recv_sem.at[i],
+                tp=tp ^ i,
+            )
+            copy.start()
+            late_copies.append(copy)
+
+    results = []
+    for s in range(2):
+        first_sums[s][0].wait_recv()
+        second_sums[s].wait_recv()
+        part = own[0, s * rows : (s + 1) * rows, :]
+        part = part + first_recv[s, 0].astype(jnp.float32)
+        results.append(part + second_recv[s].astype(jnp.float32))
+    out_ref[0] = results[0].astype(jnp.bfloat16)
+    late_total = late_send[0]
+    for copy in late_copies:
+        copy.wait_recv()
+    for i in range(1, 8):
+        late_total = late_total + late_recv[i]
+    second = results[1]
+    wide_ids = lax.broadcasted_iota(jnp.int32, second.shape, 0)
+    for j in range(moves):
+        second = jnp.where(wide_ids == slot_ref[inst, j], late_total[j : j + 1, :], second)
+    out_ref[1] = second.astype(jnp.bfloat16)
+
+    for copy in (
+        along_x
+        + along_y
+        + across
+        + to_sibling
+        + first_moves
+        + second_moves
+        + fresh_moves
+        + sibling_sums
+        + first_sums[0]
+        + first_sums[1]
+        + second_sums
+        + late_copies
+    ):
+        copy.wait_send()
+
+
+def fused(
+    x_steps, norm_gain, w_query, w_keyval, w_out, key_cache, lengths, moved_slots, partner_mask
+):
+    steps, rows, width = x_steps.shape
+    moves = moved_slots.shape[1]
+    block_len, pair_dim = key_cache.shape[2:]
+    hd = pair_dim // 2
+    q_width = w_query.shape[1]
+    heads = q_width // hd
+    both = steps * rows
+    shards_tp = norm_gain.shape[0] // width
+    bf16, f32 = jnp.bfloat16, jnp.float32
+    smem = pl.BlockSpec(memory_space=pltpu.SMEM)
+    vmem = pl.BlockSpec(memory_space=pltpu.VMEM)
+    anywhere = pl.BlockSpec(memory_space=pl.ANY)
+    dma = pltpu.SemaphoreType.DMA
+    return pl.pallas_call(
+        fused_kernel,
+        out_shape=(
+            jax.ShapeDtypeStruct((steps, rows, width), bf16),
+            jax.ShapeDtypeStruct((moves,) + key_cache.shape[1:], bf16),
+        ),
+        in_specs=[smem, smem, smem, vmem, vmem, anywhere, anywhere, anywhere, anywhere],
+        out_specs=(vmem, vmem),
+        scratch_shapes=[
+            pltpu.VMEM((8, width, q_width), bf16),
+            pltpu.VMEM((8, width, pair_dim), bf16),
+            pltpu.VMEM((8, q_width, width), bf16),
+            pltpu.VMEM((rows, block_len, pair_dim), bf16),
+            pltpu.VMEM((8, steps, rows, width), bf16),
+            pltpu.VMEM((both, q_width + pair_dim), f32),
+            pltpu.VMEM((both, 1), f32),
+            pltpu.VMEM((rows, hd), jnp.int32),
+            pltpu.VMEM((rows, 2 * heads, hd), f32),
+            pltpu.VMEM((both, pair_dim), f32),
+            pltpu.VMEM((rows, 2 * heads, hd), f32),
+            pltpu.VMEM((both, q_width), bf16),
+            pltpu.VMEM((moves, block_len, pair_dim), bf16),
+            pltpu.VMEM((moves, block_len, pair_dim), bf16),
+            pltpu.VMEM((moves, block_len, pair_dim), bf16),
+            pltpu.VMEM((moves, block_len, pair_dim), bf16),
+            pltpu.VMEM((moves, pair_dim), f32),
+            pltpu.VMEM((3, moves, pair_dim), f32),
+            pltpu.VMEM((4, both, width), bf16),
+            pltpu.VMEM((4, both, width), bf16),
+            pltpu.VMEM((2, both, width), f32),
+            pltpu.VMEM((2, 2, rows, width), bf16),
+            pltpu.VMEM((2, 2, rows, width), bf16),
+            pltpu.VMEM((2, rows, width), bf16),
+            pltpu.VMEM((2, rows, width), bf16),
+            pltpu.VMEM((moves, 2 * heads, hd), f32),
+            pltpu.VMEM((8, moves, width), f32),
+            pltpu.VMEM((8, moves, width), f32),
+            dma((25,)),
+            dma((10,)),
+            dma((10,)),
+            dma((2 * moves,)),
+            dma((2 * moves,)),
+            dma((3,)),
+            dma((3,)),
+            dma((10,)),
+            dma((10,)),
+            dma((8,)),
+            dma((8,)),
+        ],
+        compiler_params=pltpu.CompilerParams(
+            collective_id=0, has_side_effects=True, vmem_limit_bytes=60 * 2**20
+        ),
+        cost_estimate=pl.CostEstimate(
+            flops=2 * both * w_query.shape[0] * (2 * q_width + pair_dim),
+            bytes_accessed=2 * (w_query.size + w_keyval.size + w_out.size + key_cache.size),
+            transcendentals=0,
+        ),
+    )(
+        lengths,
+        moved_slots,
+        partner_mask,
+        x_steps,
+        norm_gain.reshape(shards_tp, width),
+        w_query,
+        w_keyval,
+        w_out,
+        key_cache.reshape(rows, block_len, pair_dim),
+    )
+
+
 def solution(mesh):
     placed = (
         P(None, "inst", "tp"),
@@ -206,8 +744,9 @@
         P(),
         P(),
     )
+    body = fused if mesh.shape["tp"] == KVH and mesh.shape["inst"] == 4 else shards
     return jax.shard_map(
-        shards,
+        body,
         mesh=mesh,
         in_specs=placed,
         out_specs=(P(None, "inst", "tp"), P("inst", "tp", None, None)),

time: 198 us -> 68.3 us (0.34)
  waiting for transfers between devices: 97 us -> 0 us
  Pallas kernels: 0 us -> 62.4 us
  matrix products: 53 us -> 0 us
  between operations: 14.2 us -> 0.64 us
  starting transfers between devices: 10.2 us -> 0 us
  other arithmetic: 9.54 us -> 0 us
  local copies, waits for them, and re-layouts: 13.3 us -> 4.92 us
    reduce_scatter x2 -> x0, waiting for transfers between devices: 63.7 us -> none  [decode(): lax.psum_scatter(head_terms, 'tp', scatter_dimension=1, tiled=True)]
    pallas_call x0 -> x1, Pallas kernels: none -> 62.4 us  [fused(): pl.pallas_call(fused_kernel, out_shape=(jax.ShapeDtypeStruct((steps, rows...]
    dot_general x13 -> x0, matrix products: 53 us -> none  [the longest x2 20.4 us: decode(): head_terms = jnp.dot(attended, w_out, preferred_element_type=jnp.float32)]
    ppermute x4 -> x0, waiting for transfers between devices: 33.1 us -> none  [from_partner(): return lax.ppermute(block, axis, route)]
    ppermute x4 -> x0, starting transfers between devices: 9.83 us -> none  [from_partner(): return lax.ppermute(block, axis, route)]
    gather x4 -> x0, local copies, waits for them, and re-layouts: 4.64 us -> none  [the longest x2 3.34 us: shards(): payload = (key_cache[slots_self], first_fresh[slots_self])]
    reduce_sum x4 -> x0, other arithmetic: 3.56 us -> none  [the longest x2 3.1 us: decode(): jnp.mean(widened * widened, -1, keepdims=True) + eps_norm]
    another operation x6 -> x0, other arithmetic: 3.3 us -> none  [the longest x3 2.66 us: shards(): return (jnp.stack([first_out, second_out]), arrived_rows)]
  transfers between devices with their start and end apart: 8 -> 0, of which waited for: 5 -> 0; matrix products, arithmetic and copies ran while one was open for 27% -> 0% of each run, Pallas kernels for 0% -> 0%
where the time goes in v1:
time: 68.3 us; the launch traced here: 67.9 us
  Pallas kernels  62.4 us (91%)
  local copies, waits for them, and re-layouts  4.92 us (7%)
    pallas_call x1, Pallas kernels, fused(): pl.pallas_call(fused_kernel, out_shape=(jax.ShapeDtypeStruct((steps, rows...  62.4 us
    unnamed x2, local copies, waits for them, and re-layouts  3.54 us
    reshape x1, local copies, waits for them, and re-layouts, fused(): norm_gain.reshape(shards_tp, width)  1.38 us

profile of v1, /device:TPU:0, one launch (start us, length us, event | category | flops | bytes accessed | tf_op | source)
XLA Modules:
  0.0 67.9 jit_solution(9339803640569853814)
XLA Ops:
  0.6 1.4 %reshape.10.gain_ref = f32[8,1024]{1,0:T(8,128)} reshape(f32[8192]{0:T(1024)} %param.10) | data formatting | bytes 65536 | tf_op jit(solution)/shard_map/reshape | solution.py:727
  2.0 62.4 %shard_map.104 = (bf16[2,64,1024]{2,1,0:T(8,128)(2,1)}, bf16[8,1,128,256]{3,2,1,0:T(8,128)(2,1)}) custom-call(s32[256]{0:T(256)} %len_ref.1, s32[4,8]{1,0:T(4,128)} %slot_ref.1, s32[8]{0:T(128)} %mask_ref.1, bf16[2,64,1024]{2,1,0:T(8,128)(2,1)} %x_ref.1, f32[8,1024]{1,0:T(8,128)} %reshape.10.gain_ref, bf16[8192,1024]{1,0:T(8,128)(2,1)} %wq_hbm.1, ...), custom_call_target="tpu_custom_call" | custom-call | flops 4831838208 | bytes 41943040 | tf_op jit(solution)/shard_map/pallas_call | solution.py:665
  64.4 1.7 %copy.13 = bf16[2,64,1024]{2,1,0:T(8,128)(2,1)} copy(bf16[2,64,1024]{2,1,0:T(8,128)(2,1)} %get-tuple-element.4) | data formatting | bytes 524288
  66.1 1.9 %copy.14 = bf16[8,1,128,256]{3,2,1,0:T(8,128)(2,1)} copy(bf16[8,1,128,256]{3,2,1,0:T(8,128)(2,1)} %get-tuple-element.5) | data formatting | bytes 1048576

commit v2 on v1

--- a/solution.py
+++ b/solution.py
@@ -194,6 +194,18 @@
     length_next = own_lengths.at[slots_self].set(lengths[partner * row_count + slots_partner])
     second_out, unused = decode(1, length_next + 1, cache_next, length_next, [fresh_next])
     return (jnp.stack([first_out, second_out]), arrived_rows)
+
+
+def hand_on(out_ref, arrived_ref, out_final, arrived_final, sem):
+    copies = [
+        pltpu.make_async_copy(source.at[i], target.at[i], sem.at[first + i])
+        for source, target, first in ((out_ref, out_final, 0), (arrived_ref, arrived_final, 2))
+        for i in range(source.shape[0])
+    ]
+    for copy in copies:
+        copy.start()
+    for copy in copies:
+        copy.wait()
 
 
 def fused_kernel(
@@ -224,8 +236,12 @@
     mid_in,
     mid,
     last_in,
-    fsend,
-    frecv,
+    ask_query,
+    ask_fresh,
+    asked_query,
+    asked_fresh,
+    reply,
+    replied,
     sib_send,
     sib_recv,
     own,
@@ -233,20 +249,17 @@
     first_recv,
     second_send,
     second_recv,
-    late_mixed,
-    late_send,
-    late_recv,
     load_sem,
     gather_send,
     gather_recv,
     move_send,
     move_recv,
-    fresh_send,
-    fresh_recv,
+    ask_send,
+    ask_recv,
+    reply_send,
+    reply_recv,
     sum_send,
     sum_recv,
-    late_send_sem,
-    late_recv_sem,
 ):
     tp = lax.axis_index("tp")
     inst = lax.axis_index("inst")
@@ -267,28 +280,41 @@
             device_id_type=pl.DeviceIdType.MESH,
         )
 
-    cache_load = pltpu.make_async_copy(cache_hbm, cache, load_sem.at[24])
-    cache_load.start()
+    quarter = rows // 4
+    cache_loads = [
+        pltpu.make_async_copy(
+            cache_hbm.at[pl.ds(n * quarter, quarter)],
+            cache.at[pl.ds(n * quarter, quarter)],
+            load_sem.at[24 + n],
+        )
+        for n in range(4)
+    ]
+    for load in cache_loads:
+        load.start()
     weight_loads = []
+    out_loads = []
     for i in range(8):
         start = pl.multiple_of((tp ^ i) * width, width)
-        pair = (
-            pltpu.make_async_copy(wq_hbm.at[pl.ds(start, width), :], wq.at[i], load_sem.at[i]),
+        weight_loads.append(
+            (
+                pltpu.make_async_copy(wq_hbm.at[pl.ds(start, width), :], wq.at[i], load_sem.at[i]),
+                pltpu.make_async_copy(
+                    wkv_hbm.at[pl.ds(start, width), :], wkv.at[i], load_sem.at[8 + i]
+                ),
+            )
+        )
+        out_loads.append(
             pltpu.make_async_copy(
-                wkv_hbm.at[pl.ds(start, width), :], wkv.at[i], load_sem.at[8 + i]
-            ),
-        )
-        for load in pair:
-            load.start()
-        weight_loads.append(pair)
-    out_order = (1, 3, 5, 7, 2, 6, 4, 0)
-    out_loads = {}
-    for i in out_order:
-        start = pl.multiple_of((tp ^ i) * width, width)
-        out_loads[i] = pltpu.make_async_copy(
-            wo_hbm.at[:, pl.ds(start, width)], wo.at[i], load_sem.at[16 + i]
-        )
-        out_loads[i].start()
+                wo_hbm.at[:, pl.ds(start, width)], wo.at[i], load_sem.at[16 + i]
+            )
+        )
+
+    def load_weights(*order):
+        for i in order:
+            for load in weight_loads[i]:
+                load.start()
+
+    load_weights(0)
 
     barrier = pltpu.get_barrier_semaphore()
     for i in range(1, 8):
@@ -316,7 +342,9 @@
     along_y[1].start()
     to_sibling[0].start()
 
-    cache_load.wait()
+    for load in cache_loads:
+        load.wait()
+    load_weights(1, 2, 4)
     move_bits = [(1, 2) if j < moves // 2 else (2, 1) for j in range(moves)]
     first_moves = []
     for j in range(moves):
@@ -335,11 +363,9 @@
     row_ids = lax.broadcasted_iota(jnp.int32, (rows, hd), 0)
     own_place = place[...]
     next_place = own_place
-    moved_len = []
     for j in range(moves):
         partner = inst ^ mask_ref[j]
         length = len_ref[partner * rows + slot_ref[partner, j]]
-        moved_len.append(length)
         next_place = jnp.where(row_ids == slot_ref[inst, j], length, next_place)
     positions = jnp.concatenate([own_place, next_place + 1], 0).astype(jnp.float32)
     lane = lax.broadcasted_iota(jnp.int32, (1, hd), 1)
@@ -359,16 +385,18 @@
             load.wait()
         wide = xg[i].reshape(2 * rows, width).astype(jnp.float32)
         square[...] += jnp.sum(wide * wide, -1, keepdims=True)
-        scaled = (wide * gain_ref[pl.ds(tp ^ i, 1), :]).astype(jnp.bfloat16)
-
-        @pl.loop(0, q_width // 256)
-        def _(c):
-            cols = pl.ds(pl.multiple_of(c * 256, 256), 256)
+        start = pl.multiple_of((tp ^ i) * width, width)
+        gain = gain_ref[pl.ds(start, width)]
+        scaled = (wide * gain[None, :]).astype(jnp.bfloat16)
+
+        for c in range(0, q_width, 512):
+            cols = slice(c, c + 512)
             acc[:, cols] += jnp.dot(scaled, wq[i, :, cols], preferred_element_type=jnp.float32)
 
         acc[:, q_width:] += jnp.dot(scaled, wkv[i], preferred_element_type=jnp.float32)
 
     project(0)
+    load_weights(3, 5)
     along_x[0].wait_recv()
     along_y[0].wait_recv()
     across = [feature_copy(4, 2, 6, 4, 0), feature_copy(5, 4, 6, 2, 1)]
@@ -376,6 +404,7 @@
     across[1].start()
     to_sibling[0].wait_recv()
     project(1)
+    load_weights(6, 7)
     along_x[1].wait_recv()
     to_sibling.append(feature_copy(7, 2, 3, 1))
     to_sibling[1].start()
@@ -384,10 +413,14 @@
     to_sibling[2].start()
     project(2)
     project(4)
+    for i in (1, 3, 5, 7):
+        out_loads[i].start()
     to_sibling[1].wait_recv()
     project(3)
     to_sibling[2].wait_recv()
     project(5)
+    for i in (6, 2, 4, 0):
+        out_loads[i].start()
     across[0].wait_recv()
     across[1].wait_recv()
     to_sibling.append(feature_copy(9, 6, 7, 1))
@@ -409,15 +442,134 @@
     fresh[:, :hd] = turned(acc[:, q_width : q_width + hd]).astype(jnp.float32)
     fresh[:, hd:] = (acc[:, q_width + hd :] * factor).astype(jnp.bfloat16).astype(jnp.float32)
 
+    slots = [slot_ref[inst, j] for j in range(moves)]
+    ask_query[...] = jnp.concatenate([qs[slot, heads:, :] for slot in slots], 0).astype(
+        jnp.bfloat16
+    )
     for j in range(moves):
-        fsend[pl.ds(j, 1), :] = fresh[pl.ds(slot_ref[inst, j], 1), :]
-    fresh_moves = []
-    for i in range(1, 4):
-        move = remote(
-            fsend, frecv.at[i - 1], fresh_send.at[i - 1], fresh_recv.at[i - 1], inst=inst ^ i
-        )
-        move.start()
-        fresh_moves.append(move)
+        ask_fresh[pl.ds(j, 1), :] = fresh[pl.ds(rows + slots[j], 1), :]
+    asks = []
+    for i in range(3):
+        pair = (
+            remote(
+                ask_query, asked_query.at[i], ask_send.at[i], ask_recv.at[i], inst=inst ^ (i + 1)
+            ),
+            remote(
+                ask_fresh,
+                asked_fresh.at[i],
+                ask_send.at[3 + i],
+                ask_recv.at[3 + i],
+                inst=inst ^ (i + 1),
+            ),
+        )
+        for copy in pair:
+            copy.start()
+            asks.append(copy)
+
+    def matched(mask, parts):
+        return jnp.where(mask == 1, parts[0], jnp.where(mask == 2, parts[1], parts[2]))
+
+    def attend(requests):
+        scores = [
+            scale
+            * lax.dot_general(
+                queries.astype(jnp.bfloat16),
+                keys,
+                (((1,), (1,)), ((), ())),
+                preferred_element_type=jnp.float32,
+            )
+            for queries, keys, values, length, news in requests
+        ]
+        spots = lax.broadcasted_iota(jnp.int32, scores[0].shape, 1)
+        scores = [
+            jnp.where(spots < request[3], score, floor_score)
+            for score, request in zip(scores, requests)
+        ]
+        tops = [jnp.max(score, -1, keepdims=True) for score in scores]
+        marks = []
+        for queries, keys, values, length, news in requests:
+            row_marks = []
+            for row, allowed in news:
+                mark = scale * jnp.sum(queries * row[:, :hd], -1, keepdims=True)
+                if allowed is not None:
+                    mark = jnp.where(allowed, mark, floor_score)
+                row_marks.append(mark)
+            marks.append(row_marks)
+        weights = [
+            jnp.where(spots < request[3], jnp.exp(score - top), 0.0).astype(jnp.bfloat16)
+            for score, top, request in zip(scores, tops, requests)
+        ]
+        mixes = [
+            jnp.dot(weight, request[2], preferred_element_type=jnp.float32)
+            for weight, request in zip(weights, requests)
+        ]
+        totals = [jnp.sum(weight.astype(jnp.float32), -1, keepdims=True) for weight in weights]
+        answers = []
+        for request, top, row_marks, mix, total in zip(requests, tops, marks, mixes, totals):
+            overall = reduce(jnp.maximum, row_marks, top)
+            share = jnp.exp(top - overall)
+            numerator = share * mix
+            denominator = share * total
+            for (row, allowed), mark in zip(request[4], row_marks):
+                share = jnp.exp(mark - overall)
+                if allowed is not None:
+                    share = jnp.where(allowed, share, 0.0)
+                numerator = numerator + share * row[:, hd:]
+                denominator = denominator + share
+            answers.append(numerator / denominator)
+        return answers
+
+    later = lax.broadcasted_iota(jnp.int32, (2 * heads, 1), 0) >= heads
+    batch = 16
+
+    def attend_slots(first, last):
+        @pl.loop(first, last)
+        def _(group):
+            ids = [group * batch + u for u in range(batch)]
+            answers = attend(
+                [
+                    (
+                        qs[r],
+                        cache[r, :, :hd],
+                        cache[r, :, hd:],
+                        len_ref[inst * rows + r],
+                        [(fresh[pl.ds(r, 1), :], None), (fresh[pl.ds(rows + r, 1), :], later)],
+                    )
+                    for r in ids
+                ]
+            )
+            for r, answer in zip(ids, answers):
+                mixed[r] = answer
+
+    groups = rows // batch
+    attend_slots(0, groups // 2)
+
+    for copy in asks:
+        copy.wait_recv()
+    requests = []
+    for j in range(moves):
+        slot = slots[j]
+        mask = mask_ref[j]
+        part = slice(j * heads, (j + 1) * heads)
+        queries = matched(mask, [asked_query[i].astype(jnp.float32)[part] for i in range(3)])
+        news = matched(mask, [asked_fresh[i, pl.ds(j, 1), :] for i in range(3)])
+        requests.append(
+            (
+                queries,
+                cache[slot, :, :hd],
+                cache[slot, :, hd:],
+                len_ref[inst * rows + slot],
+                [(fresh[pl.ds(slot, 1), :], None), (news, None)],
+            )
+        )
+    reply[...] = jnp.concatenate(attend(requests), 0).astype(jnp.bfloat16)
+    replies = []
+    for i in range(3):
+        copy = remote(
+            reply, replied.at[i], reply_send.at[i], reply_recv.at[i], inst=inst ^ (i + 1)
+        )
+        copy.start()
+        replies.append(copy)
 
     second_moves = []
     for j in range(moves):
@@ -434,58 +586,26 @@
         move.start()
         second_moves.append(move)
 
-    def attend(queries, keys, values, length, news):
-        score = scale * lax.dot_general(
-            queries.astype(jnp.bfloat16),
-            keys,
-            (((1,), (1,)), ((), ())),
-            preferred_element_type=jnp.float32,
-        )
-        visible = lax.broadcasted_iota(jnp.int32, score.shape, 1) < length
-        score = jnp.where(visible, score, floor_score)
-        top = jnp.max(score, -1, keepdims=True)
-        weights = jnp.where(visible, jnp.exp(score - top), 0.0).astype(jnp.bfloat16)
-        total = jnp.sum(weights.astype(jnp.float32), -1, keepdims=True)
-        mix = jnp.dot(weights, values, preferred_element_type=jnp.float32)
-        marks = []
-        overall = top
-        for row, allowed in news:
-            mark = scale * jnp.sum(queries * row[:, :hd], -1, keepdims=True)
-            if allowed is not None:
-                mark = jnp.where(allowed, mark, floor_score)
-            marks.append(mark)
-            overall = jnp.maximum(overall, mark)
-        share = jnp.exp(top - overall)
-        numerator = share * mix
-        denominator = share * total
-        for (row, allowed), mark in zip(news, marks):
-            share = jnp.exp(mark - overall)
-            if allowed is not None:
-                share = jnp.where(allowed, share, 0.0)
-            numerator = numerator + share * row[:, hd:]
-            denominator = denominator + share
-        return numerator / denominator
-
-    later = lax.broadcasted_iota(jnp.int32, (2 * heads, 1), 0) >= heads
-
-    @pl.loop(0, rows // 8)
-    def _(group):
-        for u in range(8):
-            r = group * 8 + u
-            mixed[r] = attend(
-                qs[r],
-                cache[r, :, :hd],
-                cache[r, :, hd:],
-                len_ref[inst * rows + r],
-                [(fresh[pl.ds(r, 1), :], None), (fresh[pl.ds(rows + r, 1), :], later)],
-            )
-
+    attend_slots(groups // 2, groups)
+
+    for copy in replies:
+        copy.wait_recv()
+    came = [
+        matched(
+            mask_ref[j],
+            [replied[i].astype(jnp.float32)[j * heads : (j + 1) * heads] for i in range(3)],
+        )
+        for j in range(moves)
+    ]
     for h in range(heads):
         cols = slice(h * hd, (h + 1) * hd)
         attended[:rows, cols] = mixed[:, h, :].astype(jnp.bfloat16)
-        attended[rows:, cols] = mixed[:, heads + h, :].astype(jnp.bfloat16)
-
-    tile = 256
+        second = mixed[:, heads + h, :]
+        for j in range(moves):
+            second = jnp.where(row_ids == slots[j], came[j][h : h + 1], second)
+        attended[rows:, cols] = second.astype(jnp.bfloat16)
+
+    tile = 512
 
     def column_loop(body):
         @pl.loop(0, width // tile)
@@ -567,67 +687,17 @@
         copy.start()
         second_sums.append(copy)
 
-    for move in fresh_moves:
-        move.wait_recv()
     for j in range(moves):
         second_moves[j].wait_recv()
         taken = (mask_ref[j] & move_bits[j][1]) != 0
         arrived_ref[j, 0] = jnp.where(taken, last_in[j], mid[j])
-    for j in range(moves):
-        mask = mask_ref[j]
-        carried = jnp.where(
-            mask == 1,
-            frecv[0, pl.ds(j, 1), :],
-            jnp.where(mask == 2, frecv[1, pl.ds(j, 1), :], frecv[2, pl.ds(j, 1), :]),
-        )
-        slot = slot_ref[inst, j]
-        late_mixed[j] = attend(
-            qs[slot],
-            arrived_ref[j, 0, :, :hd],
-            arrived_ref[j, 0, :, hd:],
-            moved_len[j],
-            [(carried, None), (fresh[pl.ds(rows + slot, 1), :], None)],
-        )
-    late = jnp.concatenate([late_mixed[:, heads + h, :] for h in range(heads)], -1)
-    late = late.astype(jnp.bfloat16)
-    late_copies = []
-    for i in (6, 7, 2, 3, 4, 5, 1, 0):
-
-        def body(cols):
-            late_send[i, :, cols] = jnp.dot(
-                late, wo[i, :, cols], preferred_element_type=jnp.float32
-            )
-
-        column_loop(body)
-        if i:
-            copy = remote(
-                late_send.at[i],
-                late_recv.at[i],
-                late_send_sem.at[i],
-                late_recv_sem.at[i],
-                tp=tp ^ i,
-            )
-            copy.start()
-            late_copies.append(copy)
-
-    results = []
+
     for s in range(2):
         first_sums[s][0].wait_recv()
         second_sums[s].wait_recv()
         part = own[0, s * rows : (s + 1) * rows, :]
         part = part + first_recv[s, 0].astype(jnp.float32)
-        results.append(part + second_recv[s].astype(jnp.float32))
-    out_ref[0] = results[0].astype(jnp.bfloat16)
-    late_total = late_send[0]
-    for copy in late_copies:
-        copy.wait_recv()
-    for i in range(1, 8):
-        late_total = late_total + late_recv[i]
-    second = results[1]
-    wide_ids = lax.broadcasted_iota(jnp.int32, second.shape, 0)
-    for j in range(moves):
-        second = jnp.where(wide_ids == slot_ref[inst, j], late_total[j : j + 1, :], second)
-    out_ref[1] = second.astype(jnp.bfloat16)
+        out_ref[s] = (part + second_recv[s].astype(jnp.float32)).astype(jnp.bfloat16)
 
     for copy in (
         along_x
@@ -636,12 +706,12 @@
         + to_sibling
         + first_moves
         + second_moves
-        + fresh_moves
+        + asks
+        + replies
         + sibling_sums
         + first_sums[0]
         + first_sums[1]
         + second_sums
-        + late_copies
     ):
         copy.wait_send()
 
@@ -656,13 +726,12 @@
     q_width = w_query.shape[1]
     heads = q_width // hd
     both = steps * rows
-    shards_tp = norm_gain.shape[0] // width
     bf16, f32 = jnp.bfloat16, jnp.float32
     smem = pl.BlockSpec(memory_space=pltpu.SMEM)
     vmem = pl.BlockSpec(memory_space=pltpu.VMEM)
     anywhere = pl.BlockSpec(memory_space=pl.ANY)
     dma = pltpu.SemaphoreType.DMA
-    return pl.pallas_call(
+    results = pl.pallas_call(
         fused_kernel,
         out_shape=(
             jax.ShapeDtypeStruct((steps, rows, width), bf16),
@@ -687,8 +756,12 @@
             pltpu.VMEM((moves, block_len, pair_dim), bf16),
             pltpu.VMEM((moves, block_len, pair_dim), bf16),
             pltpu.VMEM((moves, block_len, pair_dim), bf16),
+            pltpu.VMEM((moves * heads, hd), bf16),
             pltpu.VMEM((moves, pair_dim), f32),
+            pltpu.VMEM((3, moves * heads, hd), bf16),
             pltpu.VMEM((3, moves, pair_dim), f32),
+            pltpu.VMEM((moves * heads, hd), bf16),
+            pltpu.VMEM((3, moves * heads, hd), bf16),
             pltpu.VMEM((4, both, width), bf16),
             pltpu.VMEM((4, both, width), bf16),
             pltpu.VMEM((2, both, width), f32),
@@ -696,20 +769,17 @@
             pltpu.VMEM((2, 2, rows, width), bf16),
             pltpu.VMEM((2, rows, width), bf16),
             pltpu.VMEM((2, rows, width), bf16),
-            pltpu.VMEM((moves, 2 * heads, hd), f32),
-            pltpu.VMEM((8, moves, width), f32),
-            pltpu.VMEM((8, moves, width), f32),
-            dma((25,)),
+            dma((28,)),
             dma((10,)),
             dma((10,)),
             dma((2 * moves,)),
             dma((2 * moves,)),
+            dma((6,)),
+            dma((6,)),
             dma((3,)),
             dma((3,)),
             dma((10,)),
             dma((10,)),
-            dma((8,)),
-            dma((8,)),
         ],
         compiler_params=pltpu.CompilerParams(
             collective_id=0, has_side_effects=True, vmem_limit_bytes=60 * 2**20
@@ -724,12 +794,20 @@
         moved_slots,
         partner_mask,
         x_steps,
-        norm_gain.reshape(shards_tp, width),
+        norm_gain,
         w_query,
         w_keyval,
         w_out,
         key_cache.reshape(rows, block_len, pair_dim),
     )
+    return pl.pallas_call(
+        hand_on,
+        out_shape=tuple(jax.ShapeDtypeStruct(part.shape, part.dtype) for part in results),
+        in_specs=[anywhere, anywhere],
+        out_specs=(anywhere, anywhere),
+        scratch_shapes=[dma((10,))],
+        compiler_params=pltpu.CompilerParams(vmem_limit_bytes=60 * 2**20),
+    )(*results)
 
 
 def solution(mesh):

time: 68.3 us -> 74 us (1.083)
  Pallas kernels: 62.4 us -> 73 us
  local copies, waits for them, and re-layouts: 4.92 us -> 0 us
    pallas_call x0 -> x1, Pallas kernels: none -> 25 us  [fused(): pl.pallas_call(hand_on, out_shape=tuple((jax.ShapeDtypeStruct(part.shape,...]
    pallas_call x1, Pallas kernels: 62.4 us -> 48 us  [fused(): pl.pallas_call(fused_kernel, out_shape=(jax.ShapeDtypeStruct((steps, rows...]
    unnamed x2 -> x0, local copies, waits for them, and re-layouts: 3.54 us -> none
    reshape x1 -> x0, local copies, waits for them, and re-layouts: 1.38 us -> none  [fused(): norm_gain.reshape(shards_tp, width)]
where the time goes in v2:
time: 74 us; the launch traced here: 73.7 us
  Pallas kernels  73 us (99%)
    pallas_call x1, Pallas kernels, fused(): pl.pallas_call(fused_kernel, out_shape=(jax.ShapeDtypeStruct((steps, rows...  48 us
    pallas_call x1, Pallas kernels, fused(): pl.pallas_call(hand_on, out_shape=tuple((jax.ShapeDtypeStruct(part.shape,...  25 us

profile of v2, /device:TPU:0, one launch (start us, length us, event | category | flops | bytes accessed | tf_op | source)
XLA Modules:
  0.0 73.7 jit_solution(1262579449739418446)
XLA Ops:
  0.6 48.0 %shard_map.104 = (bf16[2,64,1024]{2,1,0:T(8,128)(2,1)}, bf16[8,1,128,256]{3,2,1,0:T(8,128)(2,1)}) custom-call(s32[256]{0:T(256)} %len_ref.1, s32[4,8]{1,0:T(4,128)} %slot_ref.1, s32[8]{0:T(128)} %mask_ref.1, bf16[2,64,1024]{2,1,0:T(8,128)(2,1)} %x_ref.1, f32[8192]{0:T(1024)} %gain_ref.1, bf16[8192,1024]{1,0:T(8,128)(2,1)} %wq_hbm.1, ...), custom_call_target="tpu_custom_call" | custom-call | flops 4831838208 | bytes 41943040 | tf_op jit(solution)/shard_map/pallas_call | solution.py:734
  48.6 25.0 %shard_map.105 = (bf16[2,64,1024]{2,1,0:T(8,128)(2,1)}, bf16[8,1,128,256]{3,2,1,0:T(8,128)(2,1)}) custom-call(bf16[2,64,1024]{2,1,0:T(8,128)(2,1)} %get-tuple-element.4.out_ref, bf16[8,1,128,256]{3,2,1,0:T(8,128)(2,1)} %get-tuple-element.5.arrived_ref), custom_call_target="tpu_custom_call" | custom-call | tf_op jit(solution)/shard_map/pallas_call | solution.py:803

commit v3 on v2

--- a/solution.py
+++ b/solution.py
@@ -196,16 +196,9 @@
     return (jnp.stack([first_out, second_out]), arrived_rows)
 
 
-def hand_on(out_ref, arrived_ref, out_final, arrived_final, sem):
-    copies = [
-        pltpu.make_async_copy(source.at[i], target.at[i], sem.at[first + i])
-        for source, target, first in ((out_ref, out_final, 0), (arrived_ref, arrived_final, 2))
-        for i in range(source.shape[0])
-    ]
-    for copy in copies:
-        copy.start()
-    for copy in copies:
-        copy.wait()
+def hand_on(out_ref, arrived_ref, out_final, arrived_final):
+    out_final[...] = out_ref[...]
+    arrived_final[...] = arrived_ref[...]
 
 
 def fused_kernel(
@@ -395,13 +388,13 @@
 
         acc[:, q_width:] += jnp.dot(scaled, wkv[i], preferred_element_type=jnp.float32)
 
-    project(0)
-    load_weights(3, 5)
     along_x[0].wait_recv()
     along_y[0].wait_recv()
     across = [feature_copy(4, 2, 6, 4, 0), feature_copy(5, 4, 6, 2, 1)]
     across[0].start()
     across[1].start()
+    project(0)
+    load_weights(3, 5)
     to_sibling[0].wait_recv()
     project(1)
     load_weights(6, 7)
@@ -413,13 +406,13 @@
     to_sibling[2].start()
     project(2)
     project(4)
-    for i in (1, 3, 5, 7):
+    for i in (7, 3, 6, 5):
         out_loads[i].start()
     to_sibling[1].wait_recv()
     project(3)
     to_sibling[2].wait_recv()
     project(5)
-    for i in (6, 2, 4, 0):
+    for i in (2, 1, 4, 0):
         out_loads[i].start()
     across[0].wait_recv()
     across[1].wait_recv()
@@ -542,7 +535,24 @@
                 mixed[r] = answer
 
     groups = rows // batch
-    attend_slots(0, groups // 2)
+    attend_slots(0, groups // 4)
+
+    second_moves = []
+    for j in range(moves):
+        first_moves[j].wait_recv()
+        taken = (mask_ref[j] & move_bits[j][0]) != 0
+        mid[j] = jnp.where(taken, mid_in[j], leave[j])
+        move = remote(
+            mid.at[j],
+            last_in.at[j],
+            move_send.at[moves + j],
+            move_recv.at[moves + j],
+            inst=inst ^ move_bits[j][1],
+        )
+        move.start()
+        second_moves.append(move)
+
+    attend_slots(groups // 4, groups // 2)
 
     for copy in asks:
         copy.wait_recv()
@@ -571,21 +581,6 @@
         copy.start()
         replies.append(copy)
 
-    second_moves = []
-    for j in range(moves):
-        first_moves[j].wait_recv()
-        taken = (mask_ref[j] & move_bits[j][0]) != 0
-        mid[j] = jnp.where(taken, mid_in[j], leave[j])
-        move = remote(
-            mid.at[j],
-            last_in.at[j],
-            move_send.at[moves + j],
-            move_recv.at[moves + j],
-            inst=inst ^ move_bits[j][1],
-        )
-        move.start()
-        second_moves.append(move)
-
     attend_slots(groups // 2, groups)
 
     for copy in replies:
@@ -608,27 +603,11 @@
     tile = 512
 
     def column_loop(body):
-        @pl.loop(0, width // tile)
-        def _(c):
-            body(pl.ds(pl.multiple_of(c * tile, tile), tile))
+        for c in range(0, width, tile):
+            body(slice(c, c + tile))
 
     def term(i, cols):
         return jnp.dot(attended[...], wo[i, :, cols], preferred_element_type=jnp.float32)
-
-    sibling_sums = []
-    for i in (1, 3, 5, 7):
-        k = i // 2
-        out_loads[i].wait()
-
-        def body(cols):
-            sib_send[k, :, cols] = term(i, cols).astype(jnp.bfloat16)
-
-        column_loop(body)
-        copy = remote(
-            sib_send.at[k], sib_recv.at[k], sum_send.at[k], sum_recv.at[k], tp=tp ^ 1
-        )
-        copy.start()
-        sibling_sums.append(copy)
 
     first_sums = [[None, None], [None, None]]
 
@@ -644,13 +623,19 @@
         copy.start()
         first_sums[s][n] = copy
 
-    for i in (6, 2, 4, 0):
+    sibling_sums = {}
+    for i in (7, 3, 6, 5, 2, 1, 4, 0):
         k = i // 2
         out_loads[i].wait()
-        sibling_sums[k].wait_recv()
+        if i % 2 == 0:
+            sibling_sums[k].wait_recv()
 
         def body(cols):
-            chip = term(i, cols) + sib_recv[k, :, cols].astype(jnp.float32)
+            chip = term(i, cols)
+            if i % 2:
+                sib_send[k, :, cols] = chip.astype(jnp.bfloat16)
+                return
+            chip = chip + sib_recv[k, :, cols].astype(jnp.float32)
             if i == 6:
                 first_send[0, 1, :, cols] = chip[:rows].astype(jnp.bfloat16)
                 first_send[1, 1, :, cols] = chip[rows:].astype(jnp.bfloat16)
@@ -664,7 +649,13 @@
                 own[0, :, cols] = chip
 
         column_loop(body)
-        if i == 6:
+        if i % 2:
+            copy = remote(
+                sib_send.at[k], sib_recv.at[k], sum_send.at[k], sum_recv.at[k], tp=tp ^ 1
+            )
+            copy.start()
+            sibling_sums[k] = copy
+        elif i == 6:
             send_first(0, 1)
             send_first(1, 1)
         elif i == 2:
@@ -708,7 +699,7 @@
         + second_moves
         + asks
         + replies
-        + sibling_sums
+        + list(sibling_sums.values())
         + first_sums[0]
         + first_sums[1]
         + second_sums
@@ -803,10 +794,8 @@
     return pl.pallas_call(
         hand_on,
         out_shape=tuple(jax.ShapeDtypeStruct(part.shape, part.dtype) for part in results),
-        in_specs=[anywhere, anywhere],
-        out_specs=(anywhere, anywhere),
-        scratch_shapes=[dma((10,))],
-        compiler_params=pltpu.CompilerParams(vmem_limit_bytes=60 * 2**20),
+        in_specs=[vmem, vmem],
+        out_specs=(vmem, vmem),
     )(*results)
 
 

time: 74 us -> 54.1 us (0.73)
  Pallas kernels: 73 us -> 53.3 us
    pallas_call x1, Pallas kernels: 25 us -> 2.02 us  [fused(): pl.pallas_call(hand_on, out_shape=tuple((jax.ShapeDtypeStruct(part.shape,...]
    pallas_call x1, Pallas kernels: 48 us -> 51.3 us  [fused(): pl.pallas_call(fused_kernel, out_shape=(jax.ShapeDtypeStruct((steps, rows...]
where the time goes in v3:
time: 54.1 us; the launch traced here: 53.9 us
  Pallas kernels  53.3 us (99%)
  between operations  0.64 us (1%)
    pallas_call x1, Pallas kernels, fused(): pl.pallas_call(fused_kernel, out_shape=(jax.ShapeDtypeStruct((steps, rows...  51.3 us
    pallas_call x1, Pallas kernels, fused(): pl.pallas_call(hand_on, out_shape=tuple((jax.ShapeDtypeStruct(part.shape,...  2.02 us

profile of v3, /device:TPU:0, one launch (start us, length us, event | category | flops | bytes accessed | tf_op | source)
XLA Modules:
  0.0 53.9 jit_solution(18243702502171240792)
XLA Ops:
  0.6 51.3 %shard_map.104 = (bf16[2,64,1024]{2,1,0:T(8,128)(2,1)}, bf16[8,1,128,256]{3,2,1,0:T(8,128)(2,1)}) custom-call(s32[256]{0:T(256)} %len_ref.1, s32[4,8]{1,0:T(4,128)} %slot_ref.1, s32[8]{0:T(128)} %mask_ref.1, bf16[2,64,1024]{2,1,0:T(8,128)(2,1)} %x_ref.1, f32[8192]{0:T(1024)} %gain_ref.1, bf16[8192,1024]{1,0:T(8,128)(2,1)} %wq_hbm.1, ...), custom_call_target="tpu_custom_call" | custom-call | flops 4831838208 | bytes 41943040 | tf_op jit(solution)/shard_map/pallas_call | solution.py:725
  51.9 2.0 %shard_map.105 = (bf16[2,64,1024]{2,1,0:T(8,128)(2,1)}, bf16[8,1,128,256]{3,2,1,0:T(8,128)(2,1)}) custom-call(bf16[2,64,1024]{2,1,0:T(8,128)(2,1)} %get-tuple-element.4.out_ref, bf16[8,1,128,256]{3,2,1,0:T(8,128)(2,1)} %get-tuple-element.5.arrived_ref), custom_call_target="tpu_custom_call" | custom-call | tf_op jit(solution)/shard_map/pallas_call | solution.py:794

commit v4 on v3

--- a/solution.py
+++ b/solution.py
@@ -537,21 +537,6 @@
     groups = rows // batch
     attend_slots(0, groups // 4)
 
-    second_moves = []
-    for j in range(moves):
-        first_moves[j].wait_recv()
-        taken = (mask_ref[j] & move_bits[j][0]) != 0
-        mid[j] = jnp.where(taken, mid_in[j], leave[j])
-        move = remote(
-            mid.at[j],
-            last_in.at[j],
-            move_send.at[moves + j],
-            move_recv.at[moves + j],
-            inst=inst ^ move_bits[j][1],
-        )
-        move.start()
-        second_moves.append(move)
-
     attend_slots(groups // 4, groups // 2)
 
     for copy in asks:
@@ -580,6 +565,21 @@
         )
         copy.start()
         replies.append(copy)
+
+    second_moves = []
+    for j in range(moves):
+        first_moves[j].wait_recv()
+        taken = (mask_ref[j] & move_bits[j][0]) != 0
+        mid[j] = jnp.where(taken, mid_in[j], leave[j])
+        move = remote(
+            mid.at[j],
+            last_in.at[j],
+            move_send.at[moves + j],
+            move_recv.at[moves + j],
+            inst=inst ^ move_bits[j][1],
+        )
+        move.start()
+        second_moves.append(move)
 
     attend_slots(groups // 2, groups)
 

time: 54.1 us -> 49.8 us (0.921)
  Pallas kernels: 53.3 us -> 49 us
    pallas_call x1, Pallas kernels: 51.3 us -> 47 us  [fused(): pl.pallas_call(fused_kernel, out_shape=(jax.ShapeDtypeStruct((steps, rows...]
where the time goes in v4:
time: 49.8 us; the launch traced here: 49.6 us
  Pallas kernels  49 us (98%)
  between operations  0.64 us (1%)
    pallas_call x1, Pallas kernels, fused(): pl.pallas_call(fused_kernel, out_shape=(jax.ShapeDtypeStruct((steps, rows...  47 us
    pallas_call x1, Pallas kernels, fused(): pl.pallas_call(hand_on, out_shape=tuple((jax.ShapeDtypeStruct(part.shape,...  2.02 us

profile of v4, /device:TPU:0, one launch (start us, length us, event | category | flops | bytes accessed | tf_op | source)
XLA Modules:
  0.0 49.6 jit_solution(18211663303269597277)
XLA Ops:
  0.6 47.0 %shard_map.104 = (bf16[2,64,1024]{2,1,0:T(8,128)(2,1)}, bf16[8,1,128,256]{3,2,1,0:T(8,128)(2,1)}) custom-call(s32[256]{0:T(256)} %len_ref.1, s32[4,8]{1,0:T(4,128)} %slot_ref.1, s32[8]{0:T(128)} %mask_ref.1, bf16[2,64,1024]{2,1,0:T(8,128)(2,1)} %x_ref.1, f32[8192]{0:T(1024)} %gain_ref.1, bf16[8192,1024]{1,0:T(8,128)(2,1)} %wq_hbm.1, ...), custom_call_target="tpu_custom_call" | custom-call | flops 4831838208 | bytes 41943040 | tf_op jit(solution)/shard_map/pallas_call | solution.py:725
  47.6 2.0 %shard_map.105 = (bf16[2,64,1024]{2,1,0:T(8,128)(2,1)}, bf16[8,1,128,256]{3,2,1,0:T(8,128)(2,1)}) custom-call(bf16[2,64,1024]{2,1,0:T(8,128)(2,1)} %get-tuple-element.4.out_ref, bf16[8,1,128,256]{3,2,1,0:T(8,128)(2,1)} %get-tuple-element.5.arrived_ref), custom_call_target="tpu_custom_call" | custom-call | tf_op jit(solution)/shard_map/pallas_call | solution.py:794

commit v5 on v4

--- a/solution.py
+++ b/solution.py
@@ -260,7 +260,8 @@
     width = x_ref.shape[2]
     moves = slot_ref.shape[1]
     hd = cache.shape[-1] // 2
-    heads = qs.shape[1] // 2
+    heads = qs.shape[2]
+    half = rows // 2
     scale = 1.0 / math.sqrt(hd)
 
     def remote(src, dst, send, recv, **where):
@@ -321,23 +322,49 @@
     xg[0] = x_ref[...]
     pl.semaphore_wait(barrier, 10)
 
-    def feature_copy(k, src, dst, to, part=None):
-        src_ref = xg.at[src] if part is None else xg.at[src, part]
-        dst_ref = xg.at[dst] if part is None else xg.at[dst, part]
-        return remote(src_ref, dst_ref, gather_send.at[k], gather_recv.at[k], tp=tp ^ to)
-
-    along_x = [feature_copy(0, 0, 2, 2, 0), feature_copy(1, 0, 2, 2, 1)]
-    along_y = [feature_copy(2, 0, 4, 4, 1), feature_copy(3, 0, 4, 4, 0)]
-    to_sibling = [feature_copy(6, 0, 1, 1)]
-    along_x[0].start()
-    along_y[0].start()
-    along_x[1].start()
-    along_y[1].start()
-    to_sibling[0].start()
+    def feature_copy(k, s, src, dst, to, part=slice(None)):
+        start, size = part.indices(rows)[0], len(range(*part.indices(rows)))
+        return remote(
+            xg.at[src, s, pl.ds(start, size)],
+            xg.at[dst, s, pl.ds(start, size)],
+            gather_send.at[8 * s + k],
+            gather_recv.at[8 * s + k],
+            tp=tp ^ to,
+        )
+
+    gathers = [
+        {
+            "x": feature_copy(0, s, 0, 2, 2),
+            "y": feature_copy(1, s, 0, 4, 4),
+            "xy": feature_copy(2, s, 2, 6, 4, slice(0, half)),
+            "yx": feature_copy(3, s, 4, 6, 2, slice(half, rows)),
+            1: feature_copy(4, s, 0, 1, 1),
+            3: feature_copy(5, s, 2, 3, 1),
+            5: feature_copy(6, s, 4, 5, 1),
+            7: feature_copy(7, s, 6, 7, 1),
+        }
+        for s in range(2)
+    ]
+
+    def start_gather(s):
+        for name in ("x", "y", 1):
+            gathers[s][name].start()
+
+    def forward_gather(s):
+        gathers[s]["x"].wait_recv()
+        gathers[s]["xy"].start()
+        gathers[s]["y"].wait_recv()
+        gathers[s]["yx"].start()
+
+    def share_gather(s):
+        gathers[s][3].start()
+        gathers[s][5].start()
+
+    start_gather(0)
 
     for load in cache_loads:
         load.wait()
-    load_weights(1, 2, 4)
+    load_weights(1, 2, 4, 3)
     move_bits = [(1, 2) if j < moves // 2 else (2, 1) for j in range(moves)]
     first_moves = []
     for j in range(moves):
@@ -373,91 +400,64 @@
     square[...] = jnp.zeros_like(square)
     q_width = wq.shape[2]
 
-    def project(i):
-        for load in weight_loads[i]:
-            load.wait()
-        wide = xg[i].reshape(2 * rows, width).astype(jnp.float32)
-        square[...] += jnp.sum(wide * wide, -1, keepdims=True)
+    def project(i, s):
+        if s == 0:
+            for load in weight_loads[i]:
+                load.wait()
+        part = slice(s * rows, (s + 1) * rows)
+        wide = xg[i, s].astype(jnp.float32)
+        square[part] += jnp.sum(wide * wide, -1, keepdims=True)
         start = pl.multiple_of((tp ^ i) * width, width)
         gain = gain_ref[pl.ds(start, width)]
         scaled = (wide * gain[None, :]).astype(jnp.bfloat16)
 
         for c in range(0, q_width, 512):
             cols = slice(c, c + 512)
-            acc[:, cols] += jnp.dot(scaled, wq[i, :, cols], preferred_element_type=jnp.float32)
-
-        acc[:, q_width:] += jnp.dot(scaled, wkv[i], preferred_element_type=jnp.float32)
-
-    along_x[0].wait_recv()
-    along_y[0].wait_recv()
-    across = [feature_copy(4, 2, 6, 4, 0), feature_copy(5, 4, 6, 2, 1)]
-    across[0].start()
-    across[1].start()
-    project(0)
-    load_weights(3, 5)
-    to_sibling[0].wait_recv()
-    project(1)
-    load_weights(6, 7)
-    along_x[1].wait_recv()
-    to_sibling.append(feature_copy(7, 2, 3, 1))
-    to_sibling[1].start()
-    along_y[1].wait_recv()
-    to_sibling.append(feature_copy(8, 4, 5, 1))
-    to_sibling[2].start()
-    project(2)
-    project(4)
+            acc[part, cols] += jnp.dot(scaled, wq[i, :, cols], preferred_element_type=jnp.float32)
+
+        acc[part, q_width:] += jnp.dot(scaled, wkv[i], preferred_element_type=jnp.float32)
+
+    def rotate(s):
+        part = slice(s * rows, (s + 1) * rows)
+        factor = lax.rsqrt(square[part] * (1.0 / (8 * width)) + eps_norm)
+
+        def turned(block):
+            block = block * factor
+            block = block * cosine[part] + pltpu.roll(block, hd // 2, 1) * sine[part]
+            return block.astype(jnp.bfloat16).astype(jnp.float32)
+
+        for h in range(heads):
+            qs[s, :, h, :] = turned(acc[part, h * hd : (h + 1) * hd])
+        fresh[part, :hd] = turned(acc[part, q_width : q_width + hd])
+        value = acc[part, q_width + hd :] * factor
+        fresh[part, hd:] = value.astype(jnp.bfloat16).astype(jnp.float32)
+
+    forward_gather(0)
+    start_gather(1)
+    share_gather(0)
+    project(0, 0)
+    load_weights(5, 6, 7)
+    gathers[0][1].wait_recv()
+    project(1, 0)
+    project(2, 0)
+    project(4, 0)
     for i in (7, 3, 6, 5):
         out_loads[i].start()
-    to_sibling[1].wait_recv()
-    project(3)
-    to_sibling[2].wait_recv()
-    project(5)
+    gathers[0][3].wait_recv()
+    project(3, 0)
+    gathers[0]["xy"].wait_recv()
+    gathers[0]["yx"].wait_recv()
+    gathers[0][7].start()
+    gathers[0][5].wait_recv()
+    project(5, 0)
     for i in (2, 1, 4, 0):
         out_loads[i].start()
-    across[0].wait_recv()
-    across[1].wait_recv()
-    to_sibling.append(feature_copy(9, 6, 7, 1))
-    to_sibling[3].start()
-    project(6)
-    to_sibling[3].wait_recv()
-    project(7)
-
-    factor = lax.rsqrt(square[...] * (1.0 / (8 * width)) + eps_norm)
-
-    def turned(part):
-        part = part * factor
-        return (part * cosine + pltpu.roll(part, hd // 2, 1) * sine).astype(jnp.bfloat16)
-
-    for h in range(heads):
-        rotated = turned(acc[:, h * hd : (h + 1) * hd]).astype(jnp.float32)
-        qs[:, h, :] = rotated[:rows]
-        qs[:, heads + h, :] = rotated[rows:]
-    fresh[:, :hd] = turned(acc[:, q_width : q_width + hd]).astype(jnp.float32)
-    fresh[:, hd:] = (acc[:, q_width + hd :] * factor).astype(jnp.bfloat16).astype(jnp.float32)
-
-    slots = [slot_ref[inst, j] for j in range(moves)]
-    ask_query[...] = jnp.concatenate([qs[slot, heads:, :] for slot in slots], 0).astype(
-        jnp.bfloat16
-    )
-    for j in range(moves):
-        ask_fresh[pl.ds(j, 1), :] = fresh[pl.ds(rows + slots[j], 1), :]
-    asks = []
-    for i in range(3):
-        pair = (
-            remote(
-                ask_query, asked_query.at[i], ask_send.at[i], ask_recv.at[i], inst=inst ^ (i + 1)
-            ),
-            remote(
-                ask_fresh,
-                asked_fresh.at[i],
-                ask_send.at[3 + i],
-                ask_recv.at[3 + i],
-                inst=inst ^ (i + 1),
-            ),
-        )
-        for copy in pair:
-            copy.start()
-            asks.append(copy)
+    project(6, 0)
+    gathers[0][7].wait_recv()
+    project(7, 0)
+    rotate(0)
+    forward_gather(1)
+    share_gather(1)
 
     def matched(mask, parts):
         return jnp.where(mask == 1, parts[0], jnp.where(mask == 2, parts[1], parts[2]))
@@ -512,21 +512,20 @@
             answers.append(numerator / denominator)
         return answers
 
-    later = lax.broadcasted_iota(jnp.int32, (2 * heads, 1), 0) >= heads
     batch = 16
 
-    def attend_slots(first, last):
+    def attend_slots(s, first, last):
         @pl.loop(first, last)
         def _(group):
             ids = [group * batch + u for u in range(batch)]
             answers = attend(
                 [
                     (
-                        qs[r],
+                        qs[s, r],
                         cache[r, :, :hd],
                         cache[r, :, hd:],
                         len_ref[inst * rows + r],
-                        [(fresh[pl.ds(r, 1), :], None), (fresh[pl.ds(rows + r, 1), :], later)],
+                        [(fresh[pl.ds(n * rows + r, 1), :], None) for n in range(s + 1)],
                     )
                     for r in ids
                 ]
@@ -535,9 +534,133 @@
                 mixed[r] = answer
 
     groups = rows // batch
-    attend_slots(0, groups // 4)
-
-    attend_slots(groups // 4, groups // 2)
+
+    tile = 512
+    sibling_sums = [{}, {}]
+    first_sums = [{}, {}]
+    second_sums = [[], []]
+
+    def send_first(s, n, m):
+        k = 10 * s + 4 + 2 * n + m
+        copy = remote(
+            first_send.at[s, n, m],
+            first_recv.at[s, n, m],
+            sum_send.at[k],
+            sum_recv.at[k],
+            tp=tp ^ (2, 4)[n],
+        )
+        copy.start()
+        first_sums[s][n, m] = copy
+
+    def output_block(i, s):
+        k = i // 2
+        if s == 0:
+            out_loads[i].wait()
+        if i % 2 == 0:
+            sibling_sums[s][k].wait_recv()
+        for c in range(0, width, tile):
+            cols = slice(c, c + tile)
+            chip = jnp.dot(attended[s], wo[i, :, cols], preferred_element_type=jnp.float32)
+            if i % 2:
+                sib_send[s, k, :, cols] = chip.astype(jnp.bfloat16)
+                continue
+            chip = chip + sib_recv[s, k, :, cols].astype(jnp.float32)
+            if i in (2, 6):
+                first_send[s, 0, i // 4, :, cols] = chip[:half].astype(jnp.bfloat16)
+            if i in (4, 6):
+                first_send[s, 1, int(i == 6), :, cols] = chip[half:].astype(jnp.bfloat16)
+            if i == 2:
+                own[s, 1, half:, cols] = chip[half:]
+            elif i == 4:
+                own[s, 1, :half, cols] = chip[:half]
+            elif i == 0:
+                own[s, 0, :, cols] = chip
+        if i % 2:
+            k_sem = 10 * s + k
+            copy = remote(
+                sib_send.at[s, k],
+                sib_recv.at[s, k],
+                sum_send.at[k_sem],
+                sum_recv.at[k_sem],
+                tp=tp ^ 1,
+            )
+            copy.start()
+            sibling_sums[s][k] = copy
+        if i in (2, 6):
+            send_first(s, 0, i // 4)
+        if i in (4, 6):
+            send_first(s, 1, int(i == 6))
+
+    def output(s):
+        for i in (7, 3, 6, 5, 2, 1, 4, 0):
+            output_block(i, s)
+
+    def send_second(s):
+        for n in range(2):
+            first_sums[s][n, 1].wait_recv()
+            base = own[s, 1, n * half : (n + 1) * half, :]
+            total = base + first_recv[s, n, 1].astype(jnp.float32)
+            second_send[s, n] = total.astype(jnp.bfloat16)
+            k = 10 * s + 8 + n
+            copy = remote(
+                second_send.at[s, n],
+                second_recv.at[s, n],
+                sum_send.at[k],
+                sum_recv.at[k],
+                tp=tp ^ (4, 2)[n],
+            )
+            copy.start()
+            second_sums[s].append(copy)
+
+    def finish(s):
+        for n in range(2):
+            first_sums[s][n, 0].wait_recv()
+            second_sums[s][n].wait_recv()
+            part = slice(n * half, (n + 1) * half)
+            total = own[s, 0, part, :] + first_recv[s, n, 0].astype(jnp.float32)
+            total = total + second_recv[s, n].astype(jnp.float32)
+            out_ref[s, part, :] = total.astype(jnp.bfloat16)
+
+    attend_slots(0, 0, groups)
+    for h in range(heads):
+        attended[0, :, h * hd : (h + 1) * hd] = mixed[:, h, :].astype(jnp.bfloat16)
+    output(0)
+
+    for name in (1, 3, 5, "xy", "yx"):
+        gathers[1][name].wait_recv()
+    gathers[1][7].start()
+    for i in range(7):
+        project(i, 1)
+    gathers[1][7].wait_recv()
+    project(7, 1)
+    rotate(1)
+
+    slots = [slot_ref[inst, j] for j in range(moves)]
+    ask_query[...] = jnp.concatenate([qs[1, slot] for slot in slots], 0).astype(
+        jnp.bfloat16
+    )
+    for j in range(moves):
+        ask_fresh[pl.ds(j, 1), :] = fresh[pl.ds(rows + slots[j], 1), :]
+    asks = []
+    for i in range(3):
+        pair = (
+            remote(
+                ask_query, asked_query.at[i], ask_send.at[i], ask_recv.at[i], inst=inst ^ (i + 1)
+            ),
+            remote(
+                ask_fresh,
+                asked_fresh.at[i],
+                ask_send.at[3 + i],
+                ask_recv.at[3 + i],
+                inst=inst ^ (i + 1),
+            ),
+        )
+        for copy in pair:
+            copy.start()
+            asks.append(copy)
+
+    send_second(0)
+    attend_slots(1, 0, groups // 2)
 
     for copy in asks:
         copy.wait_recv()
@@ -581,7 +704,7 @@
         move.start()
         second_moves.append(move)
 
-    attend_slots(groups // 2, groups)
+    attend_slots(1, groups // 2, groups)
 
     for copy in replies:
         copy.wait_recv()
@@ -593,116 +716,31 @@
         for j in range(moves)
     ]
     for h in range(heads):
-        cols = slice(h * hd, (h + 1) * hd)
-        attended[:rows, cols] = mixed[:, h, :].astype(jnp.bfloat16)
-        second = mixed[:, heads + h, :]
+        second = mixed[:, h, :]
         for j in range(moves):
             second = jnp.where(row_ids == slots[j], came[j][h : h + 1], second)
-        attended[rows:, cols] = second.astype(jnp.bfloat16)
-
-    tile = 512
-
-    def column_loop(body):
-        for c in range(0, width, tile):
-            body(slice(c, c + tile))
-
-    def term(i, cols):
-        return jnp.dot(attended[...], wo[i, :, cols], preferred_element_type=jnp.float32)
-
-    first_sums = [[None, None], [None, None]]
-
-    def send_first(s, n):
-        k = 4 + 2 * s + n
-        copy = remote(
-            first_send.at[s, n],
-            first_recv.at[s, n],
-            sum_send.at[k],
-            sum_recv.at[k],
-            tp=tp ^ (2, 4)[s],
-        )
-        copy.start()
-        first_sums[s][n] = copy
-
-    sibling_sums = {}
-    for i in (7, 3, 6, 5, 2, 1, 4, 0):
-        k = i // 2
-        out_loads[i].wait()
-        if i % 2 == 0:
-            sibling_sums[k].wait_recv()
-
-        def body(cols):
-            chip = term(i, cols)
-            if i % 2:
-                sib_send[k, :, cols] = chip.astype(jnp.bfloat16)
-                return
-            chip = chip + sib_recv[k, :, cols].astype(jnp.float32)
-            if i == 6:
-                first_send[0, 1, :, cols] = chip[:rows].astype(jnp.bfloat16)
-                first_send[1, 1, :, cols] = chip[rows:].astype(jnp.bfloat16)
-            elif i == 2:
-                first_send[0, 0, :, cols] = chip[:rows].astype(jnp.bfloat16)
-                own[1, :rows, cols] = chip[rows:]
-            elif i == 4:
-                own[1, rows:, cols] = chip[:rows]
-                first_send[1, 0, :, cols] = chip[rows:].astype(jnp.bfloat16)
-            else:
-                own[0, :, cols] = chip
-
-        column_loop(body)
-        if i % 2:
-            copy = remote(
-                sib_send.at[k], sib_recv.at[k], sum_send.at[k], sum_recv.at[k], tp=tp ^ 1
-            )
-            copy.start()
-            sibling_sums[k] = copy
-        elif i == 6:
-            send_first(0, 1)
-            send_first(1, 1)
-        elif i == 2:
-            send_first(0, 0)
-        elif i == 4:
-            send_first(1, 0)
-
-    second_sums = []
-    for s in range(2):
-        first_sums[s][1].wait_recv()
-        base = own[1, rows:, :] if s == 0 else own[1, :rows, :]
-        second_send[s] = (base + first_recv[s, 1].astype(jnp.float32)).astype(jnp.bfloat16)
-        copy = remote(
-            second_send.at[s],
-            second_recv.at[s],
-            sum_send.at[8 + s],
-            sum_recv.at[8 + s],
-            tp=tp ^ (4, 2)[s],
-        )
-        copy.start()
-        second_sums.append(copy)
+        attended[1, :, h * hd : (h + 1) * hd] = second.astype(jnp.bfloat16)
+    output(1)
+    finish(0)
+    send_second(1)
 
     for j in range(moves):
         second_moves[j].wait_recv()
         taken = (mask_ref[j] & move_bits[j][1]) != 0
         arrived_ref[j, 0] = jnp.where(taken, last_in[j], mid[j])
 
-    for s in range(2):
-        first_sums[s][0].wait_recv()
-        second_sums[s].wait_recv()
-        part = own[0, s * rows : (s + 1) * rows, :]
-        part = part + first_recv[s, 0].astype(jnp.float32)
-        out_ref[s] = (part + second_recv[s].astype(jnp.float32)).astype(jnp.bfloat16)
+    finish(1)
 
     for copy in (
-        along_x
-        + along_y
-        + across
-        + to_sibling
-        + first_moves
+        first_moves
         + second_moves
         + asks
         + replies
-        + list(sibling_sums.values())
-        + first_sums[0]
-        + first_sums[1]
-        + second_sums
+        + [copy for group in gathers for copy in group.values()]
+        + [copy for group in sibling_sums for copy in group.values()]
+        + [copy for group in first_sums for copy in group.values()]
+        + second_sums[0]
+        + second_sums[1]
     ):
         copy.wait_send()
 
@@ -739,10 +777,10 @@
             pltpu.VMEM((both, q_width + pair_dim), f32),
             pltpu.VMEM((both, 1), f32),
             pltpu.VMEM((rows, hd), jnp.int32),
-            pltpu.VMEM((rows, 2 * heads, hd), f32),
+            pltpu.VMEM((steps, rows, heads, hd), f32),
             pltpu.VMEM((both, pair_dim), f32),
-            pltpu.VMEM((rows, 2 * heads, hd), f32),
-            pltpu.VMEM((both, q_width), bf16),
+            pltpu.VMEM((rows, heads, hd), f32),
+            pltpu.VMEM((steps, rows, q_width), bf16),
             pltpu.VMEM((moves, block_len, pair_dim), bf16),
             pltpu.VMEM((moves, block_len, pair_dim), bf16),
             pltpu.VMEM((moves, block_len, pair_dim), bf16),
@@ -753,24 +791,24 @@
             pltpu.VMEM((3, moves, pair_dim), f32),
             pltpu.VMEM((moves * heads, hd), bf16),
             pltpu.VMEM((3, moves * heads, hd), bf16),
-            pltpu.VMEM((4, both, width), bf16),
-            pltpu.VMEM((4, both, width), bf16),
-            pltpu.VMEM((2, both, width), f32),
-            pltpu.VMEM((2, 2, rows, width), bf16),
-            pltpu.VMEM((2, 2, rows, width), bf16),
-            pltpu.VMEM((2, rows, width), bf16),
-            pltpu.VMEM((2, rows, width), bf16),
+            pltpu.VMEM((steps, 4, rows, width), bf16),
+            pltpu.VMEM((steps, 4, rows, width), bf16),
+            pltpu.VMEM((steps, 2, rows, width), f32),
+            pltpu.VMEM((steps, 2, 2, rows // 2, width), bf16),
+            pltpu.VMEM((steps, 2, 2, rows // 2, width), bf16),
+            pltpu.VMEM((steps, 2, rows // 2, width), bf16),
+            pltpu.VMEM((steps, 2, rows // 2, width), bf16),
             dma((28,)),
-            dma((10,)),
-            dma((10,)),
+            dma((16,)),
+            dma((16,)),
             dma((2 * moves,)),
             dma((2 * moves,)),
             dma((6,)),
             dma((6,)),
             dma((3,)),
             dma((3,)),
-            dma((10,)),
-            dma((10,)),
+            dma((20,)),
+            dma((20,)),
         ],
         compiler_params=pltpu.CompilerParams(
             collective_id=0, has_side_effects=True, vmem_limit_bytes=60 * 2**20

time: 49.8 us -> 56.4 us (1.13)
  Pallas kernels: 49 us -> 55.6 us
    pallas_call x1, Pallas kernels: 47 us -> 53.5 us  [fused(): pl.pallas_call(fused_kernel, out_shape=(jax.ShapeDtypeStruct((steps, rows...]
where the time goes in v5:
time: 56.4 us; the launch traced here: 56.2 us
  Pallas kernels  55.6 us (99%)
  between operations  0.64 us (1%)
    pallas_call x1, Pallas kernels, fused(): pl.pallas_call(fused_kernel, out_shape=(jax.ShapeDtypeStruct((steps, rows...  53.5 us
    pallas_call x1, Pallas kernels, fused(): pl.pallas_call(hand_on, out_shape=tuple((jax.ShapeDtypeStruct(part.shape,...  2.02 us

profile of v5, /device:TPU:0, one launch (start us, length us, event | category | flops | bytes accessed | tf_op | source)
XLA Modules:
  0.0 56.2 jit_solution(821452475541172400)
XLA Ops:
  0.6 53.5 %shard_map.104 = (bf16[2,64,1024]{2,1,0:T(8,128)(2,1)}, bf16[8,1,128,256]{3,2,1,0:T(8,128)(2,1)}) custom-call(s32[256]{0:T(256)} %len_ref.1, s32[4,8]{1,0:T(4,128)} %slot_ref.1, s32[8]{0:T(128)} %mask_ref.1, bf16[2,64,1024]{2,1,0:T(8,128)(2,1)} %x_ref.1, f32[8192]{0:T(1024)} %gain_ref.1, bf16[8192,1024]{1,0:T(8,128)(2,1)} %wq_hbm.1, ...), custom_call_target="tpu_custom_call" | custom-call | flops 4831838208 | bytes 41943040 | tf_op jit(solution)/shard_map/pallas_call | solution.py:763
  54.2 2.0 %shard_map.105 = (bf16[2,64,1024]{2,1,0:T(8,128)(2,1)}, bf16[8,1,128,256]{3,2,1,0:T(8,128)(2,1)}) custom-call(bf16[2,64,1024]{2,1,0:T(8,128)(2,1)} %get-tuple-element.4.out_ref, bf16[8,1,128,256]{3,2,1,0:T(8,128)(2,1)} %get-tuple-element.5.arrived_ref), custom_call_target="tpu_custom_call" | custom-call | tf_op jit(solution)/shard_map/pallas_call | solution.py:832

commit v6 on v4

--- a/solution.py
+++ b/solution.py
@@ -339,14 +339,15 @@
         load.wait()
     load_weights(1, 2, 4)
     move_bits = [(1, 2) if j < moves // 2 else (2, 1) for j in range(moves)]
-    first_moves = []
-    for j in range(moves):
+    first_moves = {}
+    trip_order = [n + m * (moves // 2) for n in range(moves // 2) for m in range(2)]
+    for j in trip_order:
         leave[j] = cache[slot_ref[inst, j]]
         move = remote(
             leave.at[j], mid_in.at[j], move_send.at[j], move_recv.at[j], inst=inst ^ move_bits[j][0]
         )
         move.start()
-        first_moves.append(move)
+        first_moves[j] = move
 
     @pl.loop(0, rows)
     def _(r):
@@ -458,6 +459,23 @@
         for copy in pair:
             copy.start()
             asks.append(copy)
+
+    second_moves = {}
+
+    def second_trip(ids):
+        for j in ids:
+            first_moves[j].wait_recv()
+            taken = (mask_ref[j] & move_bits[j][0]) != 0
+            mid[j] = jnp.where(taken, mid_in[j], leave[j])
+            move = remote(
+                mid.at[j],
+                last_in.at[j],
+                move_send.at[moves + j],
+                move_recv.at[moves + j],
+                inst=inst ^ move_bits[j][1],
+            )
+            move.start()
+            second_moves[j] = move
 
     def matched(mask, parts):
         return jnp.where(mask == 1, parts[0], jnp.where(mask == 2, parts[1], parts[2]))
@@ -536,8 +554,9 @@
 
     groups = rows // batch
     attend_slots(0, groups // 4)
-
+    second_trip(trip_order[:2])
     attend_slots(groups // 4, groups // 2)
+    second_trip(trip_order[2:4])
 
     for copy in asks:
         copy.wait_recv()
@@ -566,20 +585,7 @@
         copy.start()
         replies.append(copy)
 
-    second_moves = []
-    for j in range(moves):
-        first_moves[j].wait_recv()
-        taken = (mask_ref[j] & move_bits[j][0]) != 0
-        mid[j] = jnp.where(taken, mid_in[j], leave[j])
-        move = remote(
-            mid.at[j],
-            last_in.at[j],
-            move_send.at[moves + j],
-            move_recv.at[moves + j],
-            inst=inst ^ move_bits[j][1],
-        )
-        move.start()
-        second_moves.append(move)
+    second_trip(trip_order[4:])
 
     attend_slots(groups // 2, groups)
 
@@ -695,8 +701,8 @@
         + along_y
         + across
         + to_sibling
-        + first_moves
-        + second_moves
+        + list(first_moves.values())
+        + list(second_moves.values())
         + asks
         + replies
         + list(sibling_sums.values())

time: 49.8 us -> 48.6 us (0.976)
  Pallas kernels: 49 us -> 47.8 us
    pallas_call x1, Pallas kernels: 47 us -> 45.8 us  [fused(): pl.pallas_call(fused_kernel, out_shape=(jax.ShapeDtypeStruct((steps, rows...]
where the time goes in v6:
time: 48.6 us; the launch traced here: 48.5 us
  Pallas kernels  47.8 us (98%)
  between operations  0.64 us (1%)
    pallas_call x1, Pallas kernels, fused(): pl.pallas_call(fused_kernel, out_shape=(jax.ShapeDtypeStruct((steps, rows...  45.8 us
    pallas_call x1, Pallas kernels, fused(): pl.pallas_call(hand_on, out_shape=tuple((jax.ShapeDtypeStruct(part.shape,...  2.02 us

profile of v6, /device:TPU:0, one launch (start us, length us, event | category | flops | bytes accessed | tf_op | source)
XLA Modules:
  0.0 48.5 jit_solution(14902489917310003721)
XLA Ops:
  0.6 45.8 %shard_map.104 = (bf16[2,64,1024]{2,1,0:T(8,128)(2,1)}, bf16[8,1,128,256]{3,2,1,0:T(8,128)(2,1)}) custom-call(s32[256]{0:T(256)} %len_ref.1, s32[4,8]{1,0:T(4,128)} %slot_ref.1, s32[8]{0:T(128)} %mask_ref.1, bf16[2,64,1024]{2,1,0:T(8,128)(2,1)} %x_ref.1, f32[8192]{0:T(1024)} %gain_ref.1, bf16[8192,1024]{1,0:T(8,128)(2,1)} %wq_hbm.1, ...), custom_call_target="tpu_custom_call" | custom-call | flops 4831838208 | bytes 41943040 | tf_op jit(solution)/shard_map/pallas_call | solution.py:731
  46.4 2.0 %shard_map.105 = (bf16[2,64,1024]{2,1,0:T(8,128)(2,1)}, bf16[8,1,128,256]{3,2,1,0:T(8,128)(2,1)}) custom-call(bf16[2,64,1024]{2,1,0:T(8,128)(2,1)} %get-tuple-element.4.out_ref, bf16[8,1,128,256]{3,2,1,0:T(8,128)(2,1)} %get-tuple-element.5.arrived_ref), custom_call_target="tpu_custom_call" | custom-call | tf_op jit(solution)/shard_map/pallas_call | solution.py:800

commit v7 on v6

--- a/solution.py
+++ b/solution.py
@@ -531,7 +531,7 @@
         return answers
 
     later = lax.broadcasted_iota(jnp.int32, (2 * heads, 1), 0) >= heads
-    batch = 16
+    batch = 32
 
     def attend_slots(first, last):
         @pl.loop(first, last)

time: 48.6 us -> 48.6 us (level)
  no operation moved by 1% of the time
where the time goes in v7:
time: 48.6 us; the launch traced here: 48.5 us
  Pallas kernels  47.8 us (98%)
  between operations  0.64 us (1%)
    pallas_call x1, Pallas kernels, fused(): pl.pallas_call(fused_kernel, out_shape=(jax.ShapeDtypeStruct((steps, rows...  45.8 us
    pallas_call x1, Pallas kernels, fused(): pl.pallas_call(hand_on, out_shape=tuple((jax.ShapeDtypeStruct(part.shape,...  2.02 us

profile of v7, /device:TPU:0, one launch (start us, length us, event | category | flops | bytes accessed | tf_op | source)
XLA Modules:
  0.0 48.5 jit_solution(17821577950511525407)
XLA Ops:
  0.6 45.8 %shard_map.104 = (bf16[2,64,1024]{2,1,0:T(8,128)(2,1)}, bf16[8,1,128,256]{3,2,1,0:T(8,128)(2,1)}) custom-call(s32[256]{0:T(256)} %len_ref.1, s32[4,8]{1,0:T(4,128)} %slot_ref.1, s32[8]{0:T(128)} %mask_ref.1, bf16[2,64,1024]{2,1,0:T(8,128)(2,1)} %x_ref.1, f32[8192]{0:T(1024)} %gain_ref.1, bf16[8192,1024]{1,0:T(8,128)(2,1)} %wq_hbm.1, ...), custom_call_target="tpu_custom_call" | custom-call | flops 4831838208 | bytes 41943040 | tf_op jit(solution)/shard_map/pallas_call | solution.py:731
  46.4 2.0 %shard_map.105 = (bf16[2,64,1024]{2,1,0:T(8,128)(2,1)}, bf16[8,1,128,256]{3,2,1,0:T(8,128)(2,1)}) custom-call(bf16[2,64,1024]{2,1,0:T(8,128)(2,1)} %get-tuple-element.4.out_ref, bf16[8,1,128,256]{3,2,1,0:T(8,128)(2,1)} %get-tuple-element.5.arrived_ref), custom_call_target="tpu_custom_call" | custom-call | tf_op jit(solution)/shard_map/pallas_call | solution.py:800
